TPU v7x, 32 devices: a whole 2x2x4 slice. The times are simulated.
32 devices in a mesh: section: 4 (over x, core), px: 4 (over z), py: 2 (over y).
Axes of the slice: x: 2, y: 2, z: 4, core: 2. Of those that a mesh axis runs over, the one named last changes fastest.
Arguments:
- psi: float32 [2, 32, 512, 256], P(None, None, 'px', 'py'), may hold values from -3.5 to 3.5
- disorder: int32 [32, 512, 256], P(None, 'px', 'py'), may hold values from 0 to 15
Outputs:
- psi_next: float32 [2, 32, 512, 256], P(None, 'section', 'px', 'py')
All inputs are finite; a program needn't handle non-finite values.
Results may differ from a plain program's by a relative error of at most 0.00005.
Values sent between devices are 32-bit elements; how exact they have to be, the bound alone decides.
No kernel may reach another device: no remote copies, remote signals or barrier semaphores. Data moves between devices by JAX's collectives and lax.ppermute only.
A program may use at most 128 MiB of HBM per device.

v0:
```python
import functools
import math

import jax
import jax.numpy as jnp
from jax import lax
from jax.experimental import pallas as pl
from jax.experimental.pallas import tpu as pltpu
from jax.sharding import PartitionSpec as P

LEVELS = 16
STEP = 0.05
ROTATION = 0.8
COUPLING = 0.25

ROOT_OUT = math.sqrt((3.0 + 2.0 * math.sqrt(1.2)) / 7.0)
ROOT_IN = math.sqrt((3.0 - 2.0 * math.sqrt(1.2)) / 7.0)
PAIRS = (
    (0.25 * ROOT_OUT * ROOT_OUT, (18.0 - math.sqrt(30.0)) / 36.0),
    (0.25 * ROOT_IN * ROOT_IN, (18.0 + math.sqrt(30.0)) / 36.0),
)
KAPPA = STEP * COUPLING
HALF = 0.5 * STEP
SPIN = 0.5 * STEP * ROTATION

DEEP = 3
WIDE = 3 * DEEP
LANES = 128
ROWS = 8
F32 = jnp.float32


def iota(dim):
    return lax.broadcasted_iota(jnp.int32, (ROWS, LANES), dim)


def roll(value, shift, axis):
    return pltpu.roll(value, shift % value.shape[axis] if isinstance(shift, int) else shift, axis)


def strip_lanes():
    lane = iota(1)
    slot = (lane * 57) >> 9
    return slot, lane - WIDE * slot


def level_table():
    lane = iota(1)
    table = jnp.zeros((ROWS, LANES), F32)
    for level in range(LEVELS):
        table = jnp.where(lane == level, F32(STEP * 1.5 * math.sin(2.3 * level + 0.4)), table)
    return table


def look_up(table, level):
    return jnp.take_along_axis(table, level, axis=1, mode="promise_in_bounds")


def to_level(value):
    return jnp.clip(value, 0.0, LEVELS - 1.0).astype(jnp.int32)


def linear(c, xp, xm, yp, ym, zp, zm, cyp, cym, cx):
    diag = [HALF * (zp[i] + zm[i]) - (6.0 * HALF) * c[i] for i in range(2)]
    real = cyp[1] * yp[0] - cym[0] * ym[0] - cx[0] * xp[0] + cx[1] * xm[0] - diag[0]
    imag = cyp[0] * yp[1] - cym[1] * ym[1] - cx[1] * xp[1] + cx[0] * xm[1] + diag[1]
    return real, imag


def first_slope(w, lin, pot):
    g = pot + KAPPA * (w[0] * w[0] + w[1] * w[1])
    return lin[0] + g * w[1], lin[1] - g * w[0]


def second_stage(w, k, lin_w, lin_k, pot, full):
    m = [w[i] + 0.5 * k[i] for i in range(2)]
    p0 = pot + KAPPA * (m[0] * m[0] + m[1] * m[1])
    p1 = (2.0 * KAPPA) * (m[0] * k[0] + m[1] * k[1])
    p2 = KAPPA * (k[0] * k[0] + k[1] * k[1])
    n0 = [p0 * m[i] for i in range(2)]
    n1 = [p0 * k[i] + p1 * m[i] for i in range(2)]
    n2 = [p1 * k[i] + p2 * m[i] for i in range(2)]
    n3 = [p2 * k[i] for i in range(2)]
    turn = lambda n: (n[1], -n[0])
    f0 = [lin_w[i] + 0.5 * lin_k[i] + turn(n0)[i] for i in range(2)]
    f1 = [lin_k[i] + turn(n1)[i] for i in range(2)]
    f2 = turn(n2)
    f3 = turn(n3)
    base = [w[i] + 0.5 * f0[i] + (1.0 / 24.0) * f2[i] for i in range(2)]
    z = [base[i] - (1.0 / 12.0) * f1[i] - (1.0 / 80.0) * f3[i] for i in range(2)]
    if not full:
        return z, None
    total = [pot * z[i] for i in range(2)]
    for sq, weight in PAIRS:
        even = [base[i] + (0.5 * sq - 0.125) * f1[i] + (0.25 * sq * sq - 1.0 / 64.0) * f3[i] for i in range(2)]
        odd = [f0[i] + (sq / 3.0) * f2[i] for i in range(2)]
        scale = weight * KAPPA
        p = scale * (even[0] * even[0] + even[1] * even[1]) + (scale * sq) * (odd[0] * odd[0] + odd[1] * odd[1])
        q = (2.0 * scale * sq) * (even[0] * odd[0] + even[1] * odd[1])
        total = [total[i] + p * even[i] + q * odd[i] for i in range(2)]
    return z, (w[0] + total[1], w[1] - total[0])


class Place:
    def __init__(self, dims):
        self.planes, self.share, self.rows, self.cols, self.npx, self.npy = dims
        self.slots = self.share + 2 * DEEP
        self.tiles = self.rows // ROWS
        self.two = self.npy == 2
        self.sides = 1 if self.two else 2
        self.z0 = lax.axis_index("section") * self.share - DEEP
        self.px = lax.axis_index("px")
        self.py = lax.axis_index("py")

    def valid(self, p):
        return (self.z0 + p >= 0) & (self.z0 + p < self.planes)

    def is_left(self, side):
        return self.py == 1 if self.two else side == 0

    def pick(self, side, left, right):
        if self.two:
            return jnp.where(self.py == 1, left, right)
        return left if side == 0 else right

    def coordinate(self, index, count):
        return (index.astype(F32) - (count - 1) / 2.0) / (count / 2.0)

    def xcoord(self, row):
        return self.coordinate(self.px * self.rows + row, self.rows * self.npx)

    def ycoord(self, col):
        return self.coordinate(self.py * self.cols + col, self.cols * self.npy)

    def zcoord(self, slot):
        return self.coordinate(self.z0 + slot, self.planes)


def unpack_rows(sub, even, first, second):
    up = jnp.where(even, second, first)
    dn = jnp.where(even, first, second)
    upper = sub >= 4
    a = jnp.where(upper, up, dn)
    b = jnp.where(upper, roll(up, 3, 0), roll(dn, -3, 0))
    level = jnp.where(upper, roll(up, -2, 0), roll(dn, 2, 0))
    return a, b, level


def rows_kernel(dims, psi, dis, first, second, vpsi, vdis, psem, dsem):
    at = Place(dims)
    ends = (pl.ds(0, ROWS), pl.ds(at.rows - ROWS, ROWS))

    def psi_copy(p, e):
        return pltpu.make_async_copy(psi.at[:, at.z0 + p, ends[e]], vpsi.at[:, p, e], psem.at[p, e])

    def dis_copy(p, e):
        return pltpu.make_async_copy(dis.at[at.z0 + p, ends[e]], vdis.at[p, e], dsem.at[p, e])

    for p in range(1, at.slots - 1):
        deep = 2 <= p < at.slots - 2

        @pl.when(at.valid(p))
        def _():
            for e in range(2):
                psi_copy(p, e).start()
                if deep:
                    dis_copy(p, e).start()

        @pl.when(jnp.logical_not(at.valid(p)))
        def _():
            vpsi[:, p] = jnp.zeros((2, 2, ROWS, LANES), F32)
            vdis[p] = jnp.zeros((2, ROWS, LANES), jnp.int32)

    sub = iota(0)
    even = at.px % 2 == 0
    for p in range(1, at.slots - 1):
        deep = 2 <= p < at.slots - 2

        @pl.when(at.valid(p))
        def _():
            for e in range(2):
                psi_copy(p, e).wait()
                if deep:
                    dis_copy(p, e).wait()

        level = [vdis[p, e].astype(F32) if deep else jnp.zeros((ROWS, LANES), F32) for e in range(2)]
        up = jnp.where(sub >= 5, vpsi[0, p, 1], jnp.where(sub >= 2, roll(vpsi[1, p, 1], -3, 0), roll(level[1], 2, 0)))
        dn = jnp.where(sub < 3, vpsi[0, p, 0], jnp.where(sub < 6, roll(vpsi[1, p, 0], 3, 0), roll(level[0], -2, 0)))
        first[p - 1] = jnp.where(even, up, dn)
        second[p - 1] = jnp.where(even, dn, up)


def columns_kernel(dims, psi, dis, *refs):
    at = Place(dims)
    own, message = refs[: at.sides], refs[at.sides : 2 * at.sides]
    vpsi, vdis, psem, dsem = refs[2 * at.sides :]

    def psi_copy(p):
        return pltpu.make_async_copy(psi.at[:, at.z0 + p], vpsi.at[:, p], psem.at[p])

    def dis_copy(p):
        return pltpu.make_async_copy(dis.at[at.z0 + p], vdis.at[p], dsem.at[p])

    for p in range(at.slots):
        @pl.when(at.valid(p))
        def _():
            psi_copy(p).start()
            dis_copy(p).start()

        @pl.when(jnp.logical_not(at.valid(p)))
        def _():
            vpsi[:, p] = jnp.zeros((2, at.rows, LANES), F32)
            vdis[p] = jnp.zeros((at.rows, LANES), jnp.int32)

    for p in range(at.slots):
        @pl.when(at.valid(p))
        def _():
            psi_copy(p).wait()
            dis_copy(p).wait()

    slot, off = strip_lanes()
    here = [slot == p for p in range(at.slots)]
    for side in range(at.sides):
        shift = at.pick(side, DEEP, LANES - at.cols + 2 * DEEP)
        back = at.pick(side, DEEP, LANES - DEEP)

        def body(j, carry):
            rows = pl.ds(pl.multiple_of(j * ROWS, ROWS), ROWS)
            strips = []
            for load in (
                lambda p: vpsi[0, p, rows, :],
                lambda p: vpsi[1, p, rows, :],
                lambda p: vdis[p, rows, :].astype(F32),
            ):
                acc = jnp.zeros((ROWS, LANES), F32)
                for p in range(at.slots):
                    acc = jnp.where(here[p], roll(load(p), shift + WIDE * p, 1), acc)
                strips.append(acc)
            for i in range(3):
                own[side][i, rows, :] = strips[i]
            message[side][rows, :] = strip_message(at, side, off, back, *strips)
            return carry

        lax.fori_loop(0, at.tiles, body, 0, unroll=2)


def strip_message(at, side, off, back, a, b, level):
    a, level = roll(a, back, 1), roll(level, LANES - back, 1)
    place = at.pick(side, 8 - off, off)
    return jnp.where(place < DEEP, a, jnp.where(place < 2 * DEEP, b, level))


def corner_kernel(dims, first, second, *refs):
    at = Place(dims)
    message = refs[: at.sides]
    outer, whole = refs[at.sides : 2 * at.sides], refs[2 * at.sides :]
    sub = iota(0)
    even = at.px % 2 == 0
    slot, off = strip_lanes()
    tiles = [unpack_rows(sub, even, first[p - 1], second[p - 1]) for p in range(1, at.slots - 1)]
    for side in range(at.sides):
        shift = at.pick(side, DEEP, LANES - at.cols + 2 * DEEP)
        back = at.pick(side, DEEP, LANES - DEEP)
        strips = []
        for i in range(3):
            acc = jnp.zeros((ROWS, LANES), F32)
            for p in range(1, at.slots - 1):
                acc = jnp.where(slot == p, roll(tiles[p - 1][i], shift + WIDE * p, 1), acc)
            strips.append(acc)
            outer[side][i] = acc
        whole[side][: at.rows] = message[side][...]
        whole[side][at.rows :] = strip_message(at, side, off, back, *strips)


def put(ref, lead, value, base):
    ref[lead + (pl.ds(base, ROWS), slice(None))] = value


def get(ref, lead, base):
    return ref[lead + (pl.ds(base, ROWS), slice(None))]


def tile_of(ref, lead, base):
    return [get(ref, (i,) + lead, base) for i in range(2)]


def x_pair(ref, lead, base, outer, end):
    if outer:
        return tile_of(ref, lead, 1), tile_of(ref, lead, end - 1)
    return tile_of(ref, lead, base + 1), tile_of(ref, lead, base - 1)


def put_field(ref, lead, values, base, outer, end):
    for i in range(2):
        put(ref, (i,) + lead, values[i], base)
        if outer:
            put(ref, (i,) + lead, values[i], end)


def step_kernel(dims, psi, dis, first, second, part, w, d, k, lw, pot, zf, coef, dist, psem, dsem):
    at = Place(dims)
    slots, tiles, rows, cols = at.slots, at.tiles, at.rows, at.cols
    end = ROWS + rows

    def psi_copy(p):
        return pltpu.make_async_copy(psi.at[:, at.z0 + p], w.at[:, p, pl.ds(ROWS, rows)], psem.at[p])

    def dis_copy(p):
        return pltpu.make_async_copy(dis.at[at.z0 + p], d.at[p - 1, pl.ds(0, rows)], dsem.at[p])

    zero_plane = jnp.zeros((2, rows + 2 * ROWS, LANES), F32)
    for p in range(slots):
        @pl.when(at.valid(p))
        def _():
            psi_copy(p).start()
            if 1 <= p < slots - 1:
                dis_copy(p).start()

        @pl.when(jnp.logical_not(at.valid(p)))
        def _():
            w[:, p] = zero_plane
            if 1 <= p < slots - 1:
                k[:, p - 1] = zero_plane
            if 2 <= p < slots - 2:
                zf[:, p - 2] = zero_plane

    sub = iota(0)
    lane = iota(1)
    table = level_table()
    even = at.px % 2 == 0
    outer_row = jnp.where(sub >= 4, sub - ROWS, rows + sub)
    global_row = at.px * rows + outer_row
    row_ok = (global_row >= 0) & (global_row < rows * at.npx)

    ys = at.ycoord(lane)
    cx = (SPIN * ys + HALF, SPIN * ys - HALF)
    has_next = jnp.where(lane < cols - 1, 1.0, 0.0)
    has_prev = jnp.where(lane > 0, 1.0, 0.0)
    for j in range(tiles + 1):
        xs = at.xcoord(outer_row if j == 0 else sub + (j - 1) * ROWS)
        here = slice(j * ROWS, (j + 1) * ROWS)
        coef[0, here] = (SPIN * xs + HALF) * has_next
        coef[1, here] = (SPIN * xs - HALF) * has_next
        coef[2, here] = (SPIN * xs + HALF) * has_prev
        coef[3, here] = (SPIN * xs - HALF) * has_prev
        dist[here] = STEP * (xs * xs + ys * ys)

    zero = jnp.zeros((ROWS, LANES), F32)
    for p in range(1, slots - 1):
        a, b, level = unpack_rows(sub, even, first[p - 1], second[p - 1])
        put_field(w, (p,), (a, b), 0, True, end)
        d[p - 1, rows : rows + ROWS, :] = to_level(level)
    for p in (0, slots - 1):
        put_field(w, (p,), (zero, zero), 0, True, end)

    def field_linear(ref, q, base, outer):
        c = tile_of(ref, (q,), base)
        xp, xm = x_pair(ref, (q,), base, outer, end)
        zp = tile_of(ref, (q + 1,), base)
        zm = tile_of(ref, (q - 1,), base)
        yp = [roll(c[i], -1, 1) for i in range(2)]
        ym = [roll(c[i], 1, 1) for i in range(2)]
        cyp = [get(coef, (i,), base) for i in (0, 1)]
        cym = [get(coef, (i,), base) for i in (2, 3)]
        return c, linear(c, xp, xm, yp, ym, zp, zm, cyp, cym, cx)

    def wait_plane(p, with_level):
        @pl.when(at.valid(p))
        def _():
            psi_copy(p).wait()

        if with_level:
            @pl.when(at.valid(p) & (p < slots - 1))
            def _():
                dis_copy(p).wait()

    wait_plane(0, False)
    wait_plane(1, True)

    def one_body(p, carry):
        wait_plane(p + 1, True)
        zp = at.zcoord(p)
        level_at = table + STEP * (zp * zp)

        @pl.when(at.valid(p))
        def _():
            for j in range(tiles + 1):
                base, outer = j * ROWS, j == 0
                c, lin = field_linear(w, p, base, outer)
                level = d[p - 1, pl.ds(base - ROWS if j else rows, ROWS), :]
                here = look_up(level_at, level) + get(dist, (), base)
                slope = first_slope(c, lin, here)
                if outer:
                    slope = [jnp.where(row_ok, s, 0.0) for s in slope]
                put_field(k, (p - 1,), slope, base, outer, end)
                put_field(lw, (p - 1,), lin, base, False, end)
                put(pot, (p - 1,), here, base)

        return carry

    lax.fori_loop(1, slots - 1, one_body, 0)

    def two_tile(p, j, full):
        base, outer = j * ROWS, j == 0
        c, lin = field_linear(k, p - 1, base, outer)
        z, rest = second_stage(
            tile_of(w, (p,), base), c, tile_of(lw, (p - 1,), base), lin, get(pot, (p - 1,), base), full and not outer
        )
        if outer:
            z = [jnp.where(row_ok, s, 0.0) for s in z]
        put_field(zf, (p - 2,), z, base, outer, end)
        if rest is not None:
            for i in range(2):
                put(part, (i, p - DEEP), rest[i], base - ROWS)

    for p in (2, slots - 3):
        @pl.when(at.valid(p))
        def _():
            for j in range(tiles + 1):
                two_tile(p, j, False)

    def two_body(p, carry):
        for j in range(tiles + 1):
            two_tile(p, j, True)
        return carry

    lax.fori_loop(DEEP, DEEP + at.share, two_body, 0)

    def three_body(p, carry):
        for j in range(1, tiles + 1):
            base = j * ROWS
            _, lin = field_linear(zf, p - 2, base, False)
            for i in range(2):
                lead = (i, p - DEEP)
                put(part, lead, get(part, lead, base - ROWS) + lin[i], base - ROWS)
        return carry

    lax.fori_loop(DEEP, DEEP + at.share, three_body, 0)


def strip_kernel(dims, part, *refs):
    at = Place(dims)
    own, outer_own, got = (refs[i * at.sides : (i + 1) * at.sides] for i in range(3))
    out, result, sw, sk, sl, sp, sz, coef, osem = refs[3 * at.sides :]
    tiles, rows, cols = at.tiles, at.rows, at.cols
    end = ROWS + rows
    sub = iota(0)
    lane = iota(1)
    slot, off = strip_lanes()
    table = level_table()
    outer_row = jnp.where(sub >= 4, sub - ROWS, rows + sub)
    inside = lambda index, count: (index >= 0) & (index < count)
    row_ok = inside(at.px * rows + outer_row, rows * at.npx)
    zs = at.zcoord(slot)

    for j in range(tiles + 1):
        xs = at.xcoord(outer_row if j == 0 else sub + (j - 1) * ROWS)
        here = slice(j * ROWS, (j + 1) * ROWS)
        coef[0, here] = SPIN * xs + HALF
        coef[1, here] = SPIN * xs - HALF
        coef[2, here] = STEP * (xs * xs)

    for side in range(at.sides):
        col = off + at.pick(side, -DEEP, cols - 2 * DEEP)
        ok = inside(at.z0 + slot, at.planes) & inside(at.py * cols + col, cols * at.npy)
        ys = at.ycoord(col)
        cx = (SPIN * ys + HALF, SPIN * ys - HALF)
        far = STEP * (zs * zs + ys * ys)
        halo = at.pick(side, off, 8 - off) < DEEP
        back_b = at.pick(side, LANES - DEEP, DEEP)
        back_d = at.pick(side, LANES - 2 * DEEP, 2 * DEEP)

        def strip_load(base, outer):
            if outer:
                new = got[side][rows:, :]
                mine = [outer_own[side][i] for i in range(3)]
            else:
                here = pl.ds(base - ROWS, ROWS)
                new = got[side][here, :]
                mine = [own[side][i, here, :] for i in range(3)]
            a = jnp.where(halo, new, mine[0])
            b = jnp.where(halo, roll(new, back_b, 1), mine[1])
            level = to_level(jnp.where(halo, roll(new, back_d, 1), mine[2]))
            put_field(sw, (side,), (a, b), base, outer, end)
            put(sp, (side,), look_up(table, level) + (far + get(coef, (2,), base)), base)

        def strip_linear(ref, base, outer):
            c = tile_of(ref, (side,), base)
            xp, xm = x_pair(ref, (side,), base, outer, end)
            yp, ym, zp, zm = [[roll(c[i], s, 1) for i in range(2)] for s in (-1, 1, -WIDE, WIDE)]
            cy = [get(coef, (i,), base) for i in (0, 1)]
            return c, linear(c, xp, xm, yp, ym, zp, zm, cy, cy, cx)

        def keep(values, outer):
            good = (ok & row_ok) if outer else ok
            return [jnp.where(good, s, 0.0) for s in values]

        def strip_one(base, outer):
            c, lin = strip_linear(sw, base, outer)
            slope = first_slope(c, lin, get(sp, (side,), base))
            put_field(sk, (side,), keep(slope, outer), base, outer, end)
            put_field(sl, (side,), lin, base, False, end)

        def strip_two(base, outer):
            c, lin = strip_linear(sk, base, outer)
            z, rest = second_stage(
                tile_of(sw, (side,), base), c, tile_of(sl, (side,), base), lin, get(sp, (side,), base), not outer
            )
            put_field(sz, (side,), keep(z, outer), base, outer, end)
            if rest is not None:
                put_field(sl, (side,), rest, base, False, end)

        for stage in (strip_load, strip_one, strip_two):
            for j in range(tiles + 1):
                stage(j * ROWS, j == 0)

    def out_copy(p):
        return pltpu.make_async_copy(result.at[:, p], out.at[:, p], osem.at[p])

    def finish(j, carry):
        base = pl.multiple_of(j * ROWS, ROWS)
        faces = []
        for side in range(at.sides):
            c = tile_of(sz, (side,), base + ROWS)
            xp, xm = x_pair(sz, (side,), base + ROWS, False, end)
            yp, ym, zp, zm = [[roll(c[i], s, 1) for i in range(2)] for s in (-1, 1, -WIDE, WIDE)]
            cy = [get(coef, (i,), base + ROWS) for i in (0, 1)]
            col = off + at.pick(side, -DEEP, cols - 2 * DEEP)
            ys = at.ycoord(col)
            lin = linear(c, xp, xm, yp, ym, zp, zm, cy, cy, (SPIN * ys + HALF, SPIN * ys - HALF))
            faces.append([get(sl, (i, side), base + ROWS) + lin[i] for i in range(2)])
        for p in range(at.share):
            for i in range(2):
                value = get(part, (i, p), base)
                for side in range(at.sides):
                    from_lane = DEEP + WIDE * (p + DEEP)
                    shift = at.pick(side, LANES - from_lane, cols - DEEP - from_lane)
                    if not at.two and side == 1:
                        shift = shift % LANES
                    elif at.two:
                        shift = jnp.where(shift < 0, shift + LANES, shift)
                    face = at.pick(side, lane, cols - 1 - lane) < DEEP
                    value = jnp.where(face, roll(faces[side][i], shift, 1), value)
                put(result, (i, p), value, base)
        return carry

    lax.fori_loop(0, tiles, finish, 0, unroll=2)
    for p in range(at.share):
        out_copy(p).start()
    for p in range(at.share):
        out_copy(p).wait()


def local(npx, npy, psi, disorder):
    planes, rows, cols = psi.shape[1:]
    share = planes // lax.axis_size("section")
    two = npy == 2
    sides = 1 if two else 2
    slots = share + 2 * DEEP
    tall = rows + ROWS
    dims = (planes, share, rows, cols, npx, npy)
    hbm = pl.BlockSpec(memory_space=pltpu.HBM)
    vmem = pl.BlockSpec(memory_space=pltpu.VMEM)
    f32 = lambda *shape: jax.ShapeDtypeStruct(shape, F32)
    scratch = lambda *shape: pltpu.VMEM(shape, F32)
    levels = lambda *shape: pltpu.VMEM(shape, jnp.int32)
    dma = lambda *shape: pltpu.SemaphoreType.DMA(shape)

    def call(kernel, name, ins, outs, out_specs, scratches, flops, moved, *args):
        return pl.pallas_call(
            functools.partial(kernel, dims),
            out_shape=outs,
            in_specs=ins,
            out_specs=out_specs,
            scratch_shapes=scratches,
            compiler_params=pltpu.CompilerParams(vmem_limit_bytes=52 * 1024 * 1024),
            cost_estimate=pl.CostEstimate(flops=flops, bytes_accessed=moved, transcendentals=0),
            name=name,
        )(*args)

    def send(value, pairs):
        return lax.ppermute(value, ("px", "py"), pairs)

    def row_pairs(start):
        found = []
        for i in range(start, npx - 1, 2):
            for j in range(npy):
                found += [(i * npy + j, (i + 1) * npy + j), ((i + 1) * npy + j, i * npy + j)]
        return found

    cells = share * rows * cols
    block = 4 * slots * rows * cols
    first, second = call(
        rows_kernel, "pack_rows", [hbm] * 2, [f32(slots - 2, ROWS, LANES)] * 2, [vmem] * 2,
        [scratch(2, slots, 2, ROWS, LANES), levels(slots, 2, ROWS, LANES), dma(slots, 2), dma(slots, 2)],
        cells // 16, block // 8, psi, disorder,
    )
    first = send(first, row_pairs(0))
    second = send(second, row_pairs(1))

    packed = call(
        columns_kernel, "pack_columns", [hbm] * 2, [f32(3, rows, LANES)] * sides + [f32(rows, LANES)] * sides,
        [vmem] * (2 * sides),
        [scratch(2, slots, rows, cols), levels(slots, rows, cols), dma(slots), dma(slots)],
        9 * cells, 3 * block, psi, disorder,
    )
    own, message = packed[:sides], packed[sides:]

    made = call(
        corner_kernel, "pack_corners", [vmem] * (2 + sides), [f32(3, ROWS, LANES)] * sides + [f32(tall, LANES)] * sides,
        [vmem] * (2 * sides), [], cells // 8, block // 16, first, second, *message,
    )
    outer, message = made[:sides], made[sides:]
    right = [(i * npy + j, i * npy + j + 1) for i in range(npx) for j in range(npy - 1)]
    left = [(b, a) for a, b in right]
    if two:
        got = [send(message[0], right + left)]
    else:
        got = [send(message[1], right), send(message[0], left)]

    field = lambda depth: scratch(2, depth, tall + ROWS, LANES)
    part = call(
        step_kernel, "step", [hbm] * 2 + [vmem] * 2, f32(2, share, rows, cols), vmem,
        [
            field(slots),
            levels(slots - 2, tall, LANES),
            field(slots - 2),
            field(slots - 2),
            scratch(slots - 2, tall, LANES),
            field(slots - 4),
            scratch(4, tall, LANES),
            scratch(tall, LANES),
            dma(slots),
            dma(slots),
        ],
        300 * cells, 4 * block, psi, disorder, first, second,
    )
    return call(
        strip_kernel, "strips", [vmem] * (1 + 3 * sides), f32(2, share, rows, cols), hbm,
        [
            scratch(2, share, rows, cols),
            field(sides),
            field(sides),
            field(sides),
            scratch(sides, tall, LANES),
            field(sides),
            scratch(3, tall, LANES),
            dma(share),
        ],
        30 * cells, 2 * block, part, *own, *outer, *got,
    )


def solution(mesh):
    in_specs = (P(None, None, "px", "py"), P(None, "px", "py"))
    out_specs = P(None, "section", "px", "py")
    run = functools.partial(local, mesh.shape["px"], mesh.shape["py"])
    return jax.shard_map(run, mesh=mesh, in_specs=in_specs, out_specs=out_specs, check_vma=False)
```

profile of v0, /device:TPU:10, one launch (start us, length us, event | category | flops | bytes accessed | tf_op | source)
XLA Modules:
  0.0 24.0 jit_solution(17760118909876008918)
XLA Ops:
  0.0 1.5 %pack_rows.1 = (f32[12,8,128]{2,1,0:T(8,128)S(1)}, f32[12,8,128]{2,1,0:T(8,128)S(1)}) custom-call(f32[2,32,128,128]{3,2,1,0:T(8,128)} %psi.5, s32[32,128,128]{2,1,0:T(8,128)} %dis.5), custom_call_target="tpu_custom_call" | custom-call | flops 8192 | bytes 114688 | tf_op jit(solution)/shard_map/pack_rows/pallas_call | solution.py:570
  1.5 0.5 %collective-permute-start = (f32[12,8,128]{2,1,0:T(8,128)S(1)}, f32[12,8,128]{2,1,0:T(8,128)S(1)}, u32[]{:S(2)}, u32[]{:S(2)}) collective-permute-start(f32[12,8,128]{2,1,0:T(8,128)S(1)} %get-tuple-element.11), channel_id=1, source_target_pairs={{0,2},{2,0},{1,3},{3,1},{4,6},{6,4},{5,7},{7,5},{8,10},{10,8},{9,1... | collective-permute-start | bytes 147464 | tf_op jit(solution)/shard_map/ppermute | solution.py:582
  2.0 4.6 %collective-permute-start.1 = (f32[12,8,128]{2,1,0:T(8,128)S(1)}, f32[12,8,128]{2,1,0:T(8,128)S(1)}, u32[]{:S(2)}, u32[]{:S(2)}) collective-permute-start(f32[12,8,128]{2,1,0:T(8,128)S(1)} %get-tuple-element.12), channel_id=1, source_target_pairs={{2,4},{4,2},{3,5},{5,3},{10,12},{12,10},{11,13},{13,11},{18,20},{2... | collective-permute-start | bytes 147464 | tf_op jit(solution)/shard_map/ppermute | solution.py:582
  6.6 3.6 %pack_columns.1 = (f32[3,128,128]{2,1,0:T(8,128)S(1)}, f32[128,128]{1,0:T(8,128)S(1)}) custom-call(f32[2,32,128,128]{3,2,1,0:T(8,128)} %psi.5, s32[32,128,128]{2,1,0:T(8,128)} %dis.5), custom_call_target="tpu_custom_call" | custom-call | flops 1179648 | bytes 2752512 | tf_op jit(solution)/shard_map/pack_columns/pallas_call | solution.py:570
  10.2 0.0 collective-permute-done.first
  10.3 0.0 collective-permute-done.1.second
  10.3 0.2 pack_corners.1
  10.4 1.5 %collective-permute-start.2 = (f32[136,128]{1,0:T(8,128)S(1)}, f32[136,128]{1,0:T(8,128)S(1)}, u32[]{:S(2)}, u32[]{:S(2)}) collective-permute-start(f32[136,128]{1,0:T(8,128)S(1)} %get-tuple-element.16), channel_id=1, source_target_pairs={{0,1},{2,3},{4,5},{6,7},{1,0},{3,2},{5,4},{7,6},{8,9},{10,11},{12,... | collective-permute-start | bytes 208904 | tf_op jit(solution)/shard_map/ppermute | solution.py:582
  12.0 8.8 %step.1.part = f32[2,8,128,128]{3,2,1,0:T(8,128)S(1)} custom-call(f32[2,32,128,128]{3,2,1,0:T(8,128)} %psi.5, s32[32,128,128]{2,1,0:T(8,128)} %dis.5, f32[12,8,128]{2,1,0:T(8,128)S(1)} %collective-permute-done.first, f32[12,8,128]{2,1,0:T(8,128)S(1)} %collective-permute-done.1.second), custom_call_target="tpu_custom_call" | custom-call | flops 39321600 | bytes 3670016 | tf_op jit(solution)/shard_map/step/pallas_call | solution.py:570
  20.8 0.0 collective-permute-done.2.refs_2_
  20.8 3.2 %strips.1 = f32[2,8,128,128]{3,2,1,0:T(8,128)} custom-call(f32[2,8,128,128]{3,2,1,0:T(8,128)S(1)} %step.1.part, f32[3,128,128]{2,1,0:T(8,128)S(1)} %get-tuple-element.13.refs_0_, f32[3,8,128]{2,1,0:T(8,128)S(1)} %get-tuple-element.15.refs_1_, f32[136,128]{1,0:T(8,128)S(1)} %collective-permute-done.2.refs_2_), custom_call_target="tpu_custom_call" | custom-call | flops 3932160 | bytes 1835008 | tf_op jit(solution)/shard_map/strips/pallas_call | solution.py:570
Async XLA Ops:
  1.5 8.8 %collective-permute-start = (f32[12,8,128]{2,1,0:T(8,128)S(1)}, f32[12,8,128]{2,1,0:T(8,128)S(1)}, u32[]{:S(2)}, u32[]{:S(2)}) collective-permute-start(f32[12,8,128]{2,1,0:T(8,128)S(1)} %get-tuple-element.11), channel_id=1, source_target_pairs={{0,2},{2,0},{1,3},{3,1},{4,6},{6,4},{5,7},{7,5},{8,10},{10,8},{9,1... | collective-permute-start | bytes 147464 | tf_op jit(solution)/shard_map/ppermute | solution.py:582
  2.0 8.3 %collective-permute-start.1 = (f32[12,8,128]{2,1,0:T(8,128)S(1)}, f32[12,8,128]{2,1,0:T(8,128)S(1)}, u32[]{:S(2)}, u32[]{:S(2)}) collective-permute-start(f32[12,8,128]{2,1,0:T(8,128)S(1)} %get-tuple-element.12), channel_id=1, source_target_pairs={{2,4},{4,2},{3,5},{5,3},{10,12},{12,10},{11,13},{13,11},{18,20},{2... | collective-permute-start | bytes 147464 | tf_op jit(solution)/shard_map/ppermute | solution.py:582
  10.4 10.3 %collective-permute-start.2 = (f32[136,128]{1,0:T(8,128)S(1)}, f32[136,128]{1,0:T(8,128)S(1)}, u32[]{:S(2)}, u32[]{:S(2)}) collective-permute-start(f32[136,128]{1,0:T(8,128)S(1)} %get-tuple-element.16), channel_id=1, source_target_pairs={{0,1},{2,3},{4,5},{6,7},{1,0},{3,2},{5,4},{7,6},{8,9},{10,11},{12,... | collective-permute-start | bytes 208904 | tf_op jit(solution)/shard_map/ppermute | solution.py:582
where the time goes:
time: 24.2 us; the launch traced here: 24 us
  Pallas kernels  17.2 us (71%)
  starting transfers between devices  6.65 us (27%)
    pallas_call x5, Pallas kernels, call(): pl.pallas_call(functools.partial(kernel, dims), out_shape=outs, in_specs=...  17.2 us
    ppermute x3, starting transfers between devices, send(): return lax.ppermute(value, ('px', 'py'), pairs)  6.65 us
  transfers between devices with their start and end apart: 3, of which 0 were waited for; matrix products, arithmetic and copies ran while one was open for 0% of the time, Pallas kernels for 52%

commit v1 on v0

--- a/solution.py
+++ b/solution.py
@@ -212,36 +212,34 @@
             vpsi[:, p] = jnp.zeros((2, at.rows, LANES), F32)
             vdis[p] = jnp.zeros((at.rows, LANES), jnp.int32)
 
-    for p in range(at.slots):
-        @pl.when(at.valid(p))
-        def _():
-            psi_copy(p).wait()
-            dis_copy(p).wait()
-
     slot, off = strip_lanes()
     here = [slot == p for p in range(at.slots)]
-    for side in range(at.sides):
-        shift = at.pick(side, DEEP, LANES - at.cols + 2 * DEEP)
-        back = at.pick(side, DEEP, LANES - DEEP)
-
-        def body(j, carry):
-            rows = pl.ds(pl.multiple_of(j * ROWS, ROWS), ROWS)
-            strips = []
-            for load in (
-                lambda p: vpsi[0, p, rows, :],
-                lambda p: vpsi[1, p, rows, :],
-                lambda p: vdis[p, rows, :].astype(F32),
-            ):
-                acc = jnp.zeros((ROWS, LANES), F32)
-                for p in range(at.slots):
-                    acc = jnp.where(here[p], roll(load(p), shift + WIDE * p, 1), acc)
-                strips.append(acc)
-            for i in range(3):
-                own[side][i, rows, :] = strips[i]
-            message[side][rows, :] = strip_message(at, side, off, back, *strips)
-            return carry
-
-        lax.fori_loop(0, at.tiles, body, 0, unroll=2)
+    third = -(-at.slots // 3)
+    for start in range(0, at.slots, third):
+        group = range(start, min(start + third, at.slots))
+        for p in group:
+            @pl.when(at.valid(p))
+            def _():
+                psi_copy(p).wait()
+                dis_copy(p).wait()
+
+        for side in range(at.sides):
+            shift = at.pick(side, DEEP, LANES - at.cols + 2 * DEEP)
+            back = at.pick(side, DEEP, LANES - DEEP)
+            for j in range(at.tiles):
+                rows = slice(j * ROWS, (j + 1) * ROWS)
+                strips = []
+                for i in range(3):
+                    acc = own[side][i, rows, :] if start else jnp.zeros((ROWS, LANES), F32)
+                    for p in group:
+                        if i == 2 and p in (0, at.slots - 1):
+                            continue
+                        value = vpsi[i, p, rows, :] if i < 2 else vdis[p, rows, :].astype(F32)
+                        acc = jnp.where(here[p], roll(value, shift + WIDE * p, 1), acc)
+                    own[side][i, rows, :] = acc
+                    strips.append(acc)
+                if group[-1] == at.slots - 1:
+                    message[side][rows, :] = strip_message(at, side, off, back, *strips)
 
 
 def strip_message(at, side, off, back, a, b, level):
@@ -320,9 +318,7 @@
         def _():
             w[:, p] = zero_plane
             if 1 <= p < slots - 1:
-                k[:, p - 1] = zero_plane
-            if 2 <= p < slots - 2:
-                zf[:, p - 2] = zero_plane
+                d[p - 1] = jnp.zeros((rows + ROWS, LANES), jnp.int32)
 
     sub = iota(0)
     lane = iota(1)
@@ -377,28 +373,19 @@
     wait_plane(0, False)
     wait_plane(1, True)
 
-    def one_body(p, carry):
-        wait_plane(p + 1, True)
-        zp = at.zcoord(p)
-        level_at = table + STEP * (zp * zp)
-
-        @pl.when(at.valid(p))
-        def _():
-            for j in range(tiles + 1):
-                base, outer = j * ROWS, j == 0
-                c, lin = field_linear(w, p, base, outer)
-                level = d[p - 1, pl.ds(base - ROWS if j else rows, ROWS), :]
-                here = look_up(level_at, level) + get(dist, (), base)
-                slope = first_slope(c, lin, here)
-                if outer:
-                    slope = [jnp.where(row_ok, s, 0.0) for s in slope]
-                put_field(k, (p - 1,), slope, base, outer, end)
-                put_field(lw, (p - 1,), lin, base, False, end)
-                put(pot, (p - 1,), here, base)
-
-        return carry
-
-    lax.fori_loop(1, slots - 1, one_body, 0)
+    def one_tile(p, j, level_at, masked):
+        base, outer = j * ROWS, j == 0
+        c, lin = field_linear(w, p, base, outer)
+        level = d[p - 1, pl.ds(base - ROWS if j else rows, ROWS), :]
+        here = look_up(level_at, level) + get(dist, (), base)
+        slope = first_slope(c, lin, here)
+        if outer:
+            slope = [jnp.where(row_ok, s, 0.0) for s in slope]
+        if masked:
+            slope = [jnp.where(at.valid(p), s, 0.0) for s in slope]
+        put_field(k, (p - 1,), slope, base, outer, end)
+        put_field(lw, (p - 1,), lin, base, False, end)
+        put(pot, (p - 1,), here, base)
 
     def two_tile(p, j, full):
         base, outer = j * ROWS, j == 0
@@ -408,34 +395,44 @@
         )
         if outer:
             z = [jnp.where(row_ok, s, 0.0) for s in z]
+        if not full:
+            z = [jnp.where(at.valid(p), s, 0.0) for s in z]
         put_field(zf, (p - 2,), z, base, outer, end)
         if rest is not None:
             for i in range(2):
                 put(part, (i, p - DEEP), rest[i], base - ROWS)
 
-    for p in (2, slots - 3):
-        @pl.when(at.valid(p))
-        def _():
-            for j in range(tiles + 1):
-                two_tile(p, j, False)
-
-    def two_body(p, carry):
+    def three_tile(p, j):
+        base = j * ROWS
+        _, lin = field_linear(zf, p - 2, base, False)
+        for i in range(2):
+            lead = (i, p - DEEP)
+            put(part, lead, get(part, lead, base - ROWS) + lin[i], base - ROWS)
+
+    def planes(p, masked, two, three):
+        wait_plane(p + 1, True)
+        zp = at.zcoord(p)
+        level_at = table + STEP * (zp * zp)
         for j in range(tiles + 1):
-            two_tile(p, j, True)
-        return carry
-
-    lax.fori_loop(DEEP, DEEP + at.share, two_body, 0)
-
-    def three_body(p, carry):
-        for j in range(1, tiles + 1):
-            base = j * ROWS
-            _, lin = field_linear(zf, p - 2, base, False)
-            for i in range(2):
-                lead = (i, p - DEEP)
-                put(part, lead, get(part, lead, base - ROWS) + lin[i], base - ROWS)
-        return carry
-
-    lax.fori_loop(DEEP, DEEP + at.share, three_body, 0)
+            one_tile(p, j, level_at, masked)
+            if two is not None:
+                two_tile(p - 1, j, two)
+            if three and j:
+                three_tile(p - 2, j)
+
+    def loop(start, stop, *what):
+        def body(p, carry):
+            planes(p, *what)
+            return carry
+
+        lax.fori_loop(start, stop, body, 0)
+
+    last = slots - 2
+    loop(1, DEEP, True, None, False)
+    planes(jnp.int32(DEEP), False, False, False)
+    planes(jnp.int32(DEEP + 1), False, True, False)
+    loop(DEEP + 2, last, True, True, True)
+    planes(jnp.int32(last), True, False, True)
 
 
 def strip_kernel(dims, part, *refs):
@@ -517,36 +514,32 @@
     def out_copy(p):
         return pltpu.make_async_copy(result.at[:, p], out.at[:, p], osem.at[p])
 
-    def finish(j, carry):
-        base = pl.multiple_of(j * ROWS, ROWS)
-        faces = []
-        for side in range(at.sides):
-            c = tile_of(sz, (side,), base + ROWS)
-            xp, xm = x_pair(sz, (side,), base + ROWS, False, end)
+    for side in range(at.sides):
+        ys = at.ycoord(off + at.pick(side, -DEEP, cols - 2 * DEEP))
+        cx = (SPIN * ys + HALF, SPIN * ys - HALF)
+        for j in range(1, tiles + 1):
+            base = j * ROWS
+            c = tile_of(sz, (side,), base)
+            xp, xm = x_pair(sz, (side,), base, False, end)
             yp, ym, zp, zm = [[roll(c[i], s, 1) for i in range(2)] for s in (-1, 1, -WIDE, WIDE)]
-            cy = [get(coef, (i,), base + ROWS) for i in (0, 1)]
-            col = off + at.pick(side, -DEEP, cols - 2 * DEEP)
-            ys = at.ycoord(col)
-            lin = linear(c, xp, xm, yp, ym, zp, zm, cy, cy, (SPIN * ys + HALF, SPIN * ys - HALF))
-            faces.append([get(sl, (i, side), base + ROWS) + lin[i] for i in range(2)])
-        for p in range(at.share):
+            cy = [get(coef, (i,), base) for i in (0, 1)]
+            lin = linear(c, xp, xm, yp, ym, zp, zm, cy, cy, cx)
+            put_field(sk, (side,), [get(sl, (i, side), base) + lin[i] for i in range(2)], base, False, end)
+
+    def finish(p, carry):
+        from_lane = DEEP + WIDE * (p + DEEP)
+        for j in range(tiles):
             for i in range(2):
-                value = get(part, (i, p), base)
+                value = get(part, (i, p), j * ROWS)
                 for side in range(at.sides):
-                    from_lane = DEEP + WIDE * (p + DEEP)
-                    shift = at.pick(side, LANES - from_lane, cols - DEEP - from_lane)
-                    if not at.two and side == 1:
-                        shift = shift % LANES
-                    elif at.two:
-                        shift = jnp.where(shift < 0, shift + LANES, shift)
+                    shift = (at.pick(side, 0, cols - DEEP) + 2 * LANES - from_lane) % LANES
                     face = at.pick(side, lane, cols - 1 - lane) < DEEP
-                    value = jnp.where(face, roll(faces[side][i], shift, 1), value)
-                put(result, (i, p), value, base)
+                    value = jnp.where(face, roll(get(sk, (i, side), (j + 1) * ROWS), shift, 1), value)
+                put(result, (i, p), value, j * ROWS)
+        out_copy(p).start()
         return carry
 
-    lax.fori_loop(0, tiles, finish, 0, unroll=2)
-    for p in range(at.share):
-        out_copy(p).start()
+    lax.fori_loop(0, at.share, finish, 0)
     for p in range(at.share):
         out_copy(p).wait()
 

time: 24.2 us -> 22 us (0.909)
  Pallas kernels: 17.2 us -> 15.1 us
    pallas_call x5, Pallas kernels: 17.2 us -> 15.1 us  [call(): pl.pallas_call(functools.partial(kernel, dims), out_shape=outs, in_specs=...]
  transfers between devices with their start and end apart: 3 -> 3, of which waited for: 0 -> 0; matrix products, arithmetic and copies ran while one was open for 0% -> 0% of each run, Pallas kernels for 52% -> 51%
where the time goes in v1:
time: 22 us; the launch traced here: 21.8 us
  Pallas kernels  15.1 us (69%)
  starting transfers between devices  6.65 us (30%)
    pallas_call x5, Pallas kernels, call(): pl.pallas_call(functools.partial(kernel, dims), out_shape=outs, in_specs=...  15.1 us
    ppermute x3, starting transfers between devices, send(): return lax.ppermute(value, ('px', 'py'), pairs)  6.65 us
  transfers between devices with their start and end apart: 3, of which 0 were waited for; matrix products, arithmetic and copies ran while one was open for 0% of the time, Pallas kernels for 51%

profile of v1, /device:TPU:10, one launch (start us, length us, event | category | flops | bytes accessed | tf_op | source)
XLA Modules:
  0.0 21.8 jit_solution(18035882921847579219)
XLA Ops:
  0.0 1.5 %pack_rows.1 = (f32[12,8,128]{2,1,0:T(8,128)S(1)}, f32[12,8,128]{2,1,0:T(8,128)S(1)}) custom-call(f32[2,32,128,128]{3,2,1,0:T(8,128)} %psi.5, s32[32,128,128]{2,1,0:T(8,128)} %dis.5), custom_call_target="tpu_custom_call" | custom-call | flops 8192 | bytes 114688 | tf_op jit(solution)/shard_map/pack_rows/pallas_call | solution.py:563
  1.5 0.5 %collective-permute-start = (f32[12,8,128]{2,1,0:T(8,128)S(1)}, f32[12,8,128]{2,1,0:T(8,128)S(1)}, u32[]{:S(2)}, u32[]{:S(2)}) collective-permute-start(f32[12,8,128]{2,1,0:T(8,128)S(1)} %get-tuple-element.11), channel_id=1, source_target_pairs={{0,2},{2,0},{1,3},{3,1},{4,6},{6,4},{5,7},{7,5},{8,10},{10,8},{9,1... | collective-permute-start | bytes 147464 | tf_op jit(solution)/shard_map/ppermute | solution.py:575
  2.0 4.6 %collective-permute-start.1 = (f32[12,8,128]{2,1,0:T(8,128)S(1)}, f32[12,8,128]{2,1,0:T(8,128)S(1)}, u32[]{:S(2)}, u32[]{:S(2)}) collective-permute-start(f32[12,8,128]{2,1,0:T(8,128)S(1)} %get-tuple-element.12), channel_id=1, source_target_pairs={{2,4},{4,2},{3,5},{5,3},{10,12},{12,10},{11,13},{13,11},{18,20},{2... | collective-permute-start | bytes 147464 | tf_op jit(solution)/shard_map/ppermute | solution.py:575
  6.6 2.9 %pack_columns.1 = (f32[3,128,128]{2,1,0:T(8,128)S(1)}, f32[128,128]{1,0:T(8,128)S(1)}) custom-call(f32[2,32,128,128]{3,2,1,0:T(8,128)} %psi.5, s32[32,128,128]{2,1,0:T(8,128)} %dis.5), custom_call_target="tpu_custom_call" | custom-call | flops 1179648 | bytes 2752512 | tf_op jit(solution)/shard_map/pack_columns/pallas_call | solution.py:563
  9.5 0.0 collective-permute-done.first
  9.5 0.0 collective-permute-done.1.second
  9.5 0.2 pack_corners.1
  9.7 1.5 %collective-permute-start.2 = (f32[136,128]{1,0:T(8,128)S(1)}, f32[136,128]{1,0:T(8,128)S(1)}, u32[]{:S(2)}, u32[]{:S(2)}) collective-permute-start(f32[136,128]{1,0:T(8,128)S(1)} %get-tuple-element.16), channel_id=1, source_target_pairs={{0,1},{2,3},{4,5},{6,7},{1,0},{3,2},{5,4},{7,6},{8,9},{10,11},{12,... | collective-permute-start | bytes 208904 | tf_op jit(solution)/shard_map/ppermute | solution.py:575
  11.2 8.2 %step.1.part = f32[2,8,128,128]{3,2,1,0:T(8,128)S(1)} custom-call(f32[2,32,128,128]{3,2,1,0:T(8,128)} %psi.5, s32[32,128,128]{2,1,0:T(8,128)} %dis.5, f32[12,8,128]{2,1,0:T(8,128)S(1)} %collective-permute-done.first, f32[12,8,128]{2,1,0:T(8,128)S(1)} %collective-permute-done.1.second), custom_call_target="tpu_custom_call" | custom-call | flops 39321600 | bytes 3670016 | tf_op jit(solution)/shard_map/step/pallas_call | solution.py:563
  19.4 0.0 collective-permute-done.2.refs_2_
  19.4 2.4 %strips.1 = f32[2,8,128,128]{3,2,1,0:T(8,128)} custom-call(f32[2,8,128,128]{3,2,1,0:T(8,128)S(1)} %step.1.part, f32[3,128,128]{2,1,0:T(8,128)S(1)} %get-tuple-element.13.refs_0_, f32[3,8,128]{2,1,0:T(8,128)S(1)} %get-tuple-element.15.refs_1_, f32[136,128]{1,0:T(8,128)S(1)} %collective-permute-done.2.refs_2_), custom_call_target="tpu_custom_call" | custom-call | flops 3932160 | bytes 1835008 | tf_op jit(solution)/shard_map/strips/pallas_call | solution.py:563
Async XLA Ops:
  1.5 8.0 %collective-permute-start = (f32[12,8,128]{2,1,0:T(8,128)S(1)}, f32[12,8,128]{2,1,0:T(8,128)S(1)}, u32[]{:S(2)}, u32[]{:S(2)}) collective-permute-start(f32[12,8,128]{2,1,0:T(8,128)S(1)} %get-tuple-element.11), channel_id=1, source_target_pairs={{0,2},{2,0},{1,3},{3,1},{4,6},{6,4},{5,7},{7,5},{8,10},{10,8},{9,1... | collective-permute-start | bytes 147464 | tf_op jit(solution)/shard_map/ppermute | solution.py:575
  2.0 7.5 %collective-permute-start.1 = (f32[12,8,128]{2,1,0:T(8,128)S(1)}, f32[12,8,128]{2,1,0:T(8,128)S(1)}, u32[]{:S(2)}, u32[]{:S(2)}) collective-permute-start(f32[12,8,128]{2,1,0:T(8,128)S(1)} %get-tuple-element.12), channel_id=1, source_target_pairs={{2,4},{4,2},{3,5},{5,3},{10,12},{12,10},{11,13},{13,11},{18,20},{2... | collective-permute-start | bytes 147464 | tf_op jit(solution)/shard_map/ppermute | solution.py:575
  9.7 9.7 %collective-permute-start.2 = (f32[136,128]{1,0:T(8,128)S(1)}, f32[136,128]{1,0:T(8,128)S(1)}, u32[]{:S(2)}, u32[]{:S(2)}) collective-permute-start(f32[136,128]{1,0:T(8,128)S(1)} %get-tuple-element.16), channel_id=1, source_target_pairs={{0,1},{2,3},{4,5},{6,7},{1,0},{3,2},{5,4},{7,6},{8,9},{10,11},{12,... | collective-permute-start | bytes 208904 | tf_op jit(solution)/shard_map/ppermute | solution.py:575

commit v2 on v1

--- a/solution.py
+++ b/solution.py
@@ -115,6 +115,9 @@
     def valid(self, p):
         return (self.z0 + p >= 0) & (self.z0 + p < self.planes)
 
+    def plane(self, p):
+        return jnp.clip(self.z0 + p, 0, self.planes - 1)
+
     def is_left(self, side):
         return self.py == 1 if self.two else side == 0
 
@@ -148,98 +151,62 @@
 
 def rows_kernel(dims, psi, dis, first, second, vpsi, vdis, psem, dsem):
     at = Place(dims)
-    ends = (pl.ds(0, ROWS), pl.ds(at.rows - ROWS, ROWS))
-
-    def psi_copy(p, e):
-        return pltpu.make_async_copy(psi.at[:, at.z0 + p, ends[e]], vpsi.at[:, p, e], psem.at[p, e])
-
-    def dis_copy(p, e):
-        return pltpu.make_async_copy(dis.at[at.z0 + p, ends[e]], vdis.at[p, e], dsem.at[p, e])
-
-    for p in range(1, at.slots - 1):
-        deep = 2 <= p < at.slots - 2
-
-        @pl.when(at.valid(p))
-        def _():
-            for e in range(2):
-                psi_copy(p, e).start()
-                if deep:
-                    dis_copy(p, e).start()
-
-        @pl.when(jnp.logical_not(at.valid(p)))
-        def _():
-            vpsi[:, p] = jnp.zeros((2, 2, ROWS, LANES), F32)
-            vdis[p] = jnp.zeros((2, ROWS, LANES), jnp.int32)
-
+    count = at.slots - 2
+    start = at.z0 + 1
+    window = jnp.clip(start, 0, at.planes - count)
+    span = pl.ds(window, count)
+    copies = []
+    for e, edge in enumerate((pl.ds(0, ROWS), pl.ds(at.rows - ROWS, ROWS))):
+        copies.append(pltpu.make_async_copy(psi.at[:, span, edge], vpsi.at[e], psem.at[e]))
+        copies.append(pltpu.make_async_copy(dis.at[span, edge], vdis.at[e], dsem.at[e]))
+    for copy in copies:
+        copy.start()
     sub = iota(0)
     even = at.px % 2 == 0
-    for p in range(1, at.slots - 1):
-        deep = 2 <= p < at.slots - 2
-
-        @pl.when(at.valid(p))
-        def _():
-            for e in range(2):
-                psi_copy(p, e).wait()
-                if deep:
-                    dis_copy(p, e).wait()
-
-        level = [vdis[p, e].astype(F32) if deep else jnp.zeros((ROWS, LANES), F32) for e in range(2)]
-        up = jnp.where(sub >= 5, vpsi[0, p, 1], jnp.where(sub >= 2, roll(vpsi[1, p, 1], -3, 0), roll(level[1], 2, 0)))
-        dn = jnp.where(sub < 3, vpsi[0, p, 0], jnp.where(sub < 6, roll(vpsi[1, p, 0], 3, 0), roll(level[0], -2, 0)))
-        first[p - 1] = jnp.where(even, up, dn)
-        second[p - 1] = jnp.where(even, dn, up)
-
-
-def columns_kernel(dims, psi, dis, *refs):
+    for copy in copies:
+        copy.wait()
+    for t in range(count):
+        z = start + t
+        index = jnp.clip(z - window, 0, count - 1)
+        inside = (z >= 0) & (z < at.planes)
+        a, b = [[vpsi[e, i, index] for e in range(2)] for i in range(2)]
+        level = [vdis[e, index].astype(F32) for e in range(2)]
+        up = jnp.where(sub >= 5, a[1], jnp.where(sub >= 2, roll(b[1], -3, 0), roll(level[1], 2, 0)))
+        dn = jnp.where(sub < 3, a[0], jnp.where(sub < 6, roll(b[0], 3, 0), roll(level[0], -2, 0)))
+        first[t] = jnp.where(inside, jnp.where(even, up, dn), 0.0)
+        second[t] = jnp.where(inside, jnp.where(even, dn, up), 0.0)
+
+
+def columns_kernel(dims, psi, dis, pot, *refs):
     at = Place(dims)
-    own, message = refs[: at.sides], refs[at.sides : 2 * at.sides]
-    vpsi, vdis, psem, dsem = refs[2 * at.sides :]
-
-    def psi_copy(p):
-        return pltpu.make_async_copy(psi.at[:, at.z0 + p], vpsi.at[:, p], psem.at[p])
-
-    def dis_copy(p):
-        return pltpu.make_async_copy(dis.at[at.z0 + p], vdis.at[p], dsem.at[p])
-
-    for p in range(at.slots):
-        @pl.when(at.valid(p))
-        def _():
-            psi_copy(p).start()
-            dis_copy(p).start()
-
-        @pl.when(jnp.logical_not(at.valid(p)))
-        def _():
-            vpsi[:, p] = jnp.zeros((2, at.rows, LANES), F32)
-            vdis[p] = jnp.zeros((at.rows, LANES), jnp.int32)
-
+    own, message = refs[: at.sides], refs[at.sides :]
     slot, off = strip_lanes()
-    here = [slot == p for p in range(at.slots)]
-    third = -(-at.slots // 3)
-    for start in range(0, at.slots, third):
-        group = range(start, min(start + third, at.slots))
-        for p in group:
-            @pl.when(at.valid(p))
-            def _():
-                psi_copy(p).wait()
-                dis_copy(p).wait()
-
+    sub = iota(0)
+    table = level_table()
+    ys = at.ycoord(iota(1))
+    here = [slot == jnp.where(at.valid(p), p, -1) for p in range(at.slots)]
+    level_at = [table + STEP * (at.zcoord(p) * at.zcoord(p)) for p in range(at.slots)]
+    for j in range(at.tiles):
+        rows = slice(j * ROWS, (j + 1) * ROWS)
+        xs = at.xcoord(sub + j * ROWS)
+        dist = STEP * (xs * xs + ys * ys)
+        for p in range(1, at.slots - 1):
+            pot[p - 1, rows, :] = look_up(level_at[p], dis[at.plane(p), rows, :]) + dist
         for side in range(at.sides):
             shift = at.pick(side, DEEP, LANES - at.cols + 2 * DEEP)
             back = at.pick(side, DEEP, LANES - DEEP)
-            for j in range(at.tiles):
-                rows = slice(j * ROWS, (j + 1) * ROWS)
-                strips = []
-                for i in range(3):
-                    acc = own[side][i, rows, :] if start else jnp.zeros((ROWS, LANES), F32)
-                    for p in group:
-                        if i == 2 and p in (0, at.slots - 1):
-                            continue
-                        value = vpsi[i, p, rows, :] if i < 2 else vdis[p, rows, :].astype(F32)
-                        acc = jnp.where(here[p], roll(value, shift + WIDE * p, 1), acc)
-                    own[side][i, rows, :] = acc
-                    strips.append(acc)
-                if group[-1] == at.slots - 1:
-                    message[side][rows, :] = strip_message(at, side, off, back, *strips)
+            strips = []
+            for i in range(3):
+                acc = jnp.zeros((ROWS, LANES), F32)
+                for p in range(at.slots):
+                    if i == 2 and p in (0, at.slots - 1):
+                        continue
+                    z = at.plane(p)
+                    value = psi[i, z, rows, :] if i < 2 else dis[z, rows, :].astype(F32)
+                    acc = jnp.where(here[p], roll(value, shift + WIDE * p, 1), acc)
+                own[side][i, rows, :] = acc
+                strips.append(acc)
+            message[side][rows, :] = strip_message(at, side, off, back, *strips)
 
 
 def strip_message(at, side, off, back, a, b, level):
@@ -295,31 +262,10 @@
             put(ref, (i,) + lead, values[i], end)
 
 
-def step_kernel(dims, psi, dis, first, second, part, w, d, k, lw, pot, zf, coef, dist, psem, dsem):
+def step_kernel(dims, psi, pot, first, second, part, w, k, lw, outer_pot, zf, coef):
     at = Place(dims)
     slots, tiles, rows, cols = at.slots, at.tiles, at.rows, at.cols
     end = ROWS + rows
-
-    def psi_copy(p):
-        return pltpu.make_async_copy(psi.at[:, at.z0 + p], w.at[:, p, pl.ds(ROWS, rows)], psem.at[p])
-
-    def dis_copy(p):
-        return pltpu.make_async_copy(dis.at[at.z0 + p], d.at[p - 1, pl.ds(0, rows)], dsem.at[p])
-
-    zero_plane = jnp.zeros((2, rows + 2 * ROWS, LANES), F32)
-    for p in range(slots):
-        @pl.when(at.valid(p))
-        def _():
-            psi_copy(p).start()
-            if 1 <= p < slots - 1:
-                dis_copy(p).start()
-
-        @pl.when(jnp.logical_not(at.valid(p)))
-        def _():
-            w[:, p] = zero_plane
-            if 1 <= p < slots - 1:
-                d[p - 1] = jnp.zeros((rows + ROWS, LANES), jnp.int32)
-
     sub = iota(0)
     lane = iota(1)
     table = level_table()
@@ -339,13 +285,15 @@
         coef[1, here] = (SPIN * xs - HALF) * has_next
         coef[2, here] = (SPIN * xs + HALF) * has_prev
         coef[3, here] = (SPIN * xs - HALF) * has_prev
-        dist[here] = STEP * (xs * xs + ys * ys)
 
     zero = jnp.zeros((ROWS, LANES), F32)
+    xs = at.xcoord(outer_row)
+    dist = STEP * (xs * xs + ys * ys)
     for p in range(1, slots - 1):
         a, b, level = unpack_rows(sub, even, first[p - 1], second[p - 1])
         put_field(w, (p,), (a, b), 0, True, end)
-        d[p - 1, rows : rows + ROWS, :] = to_level(level)
+        zs = at.zcoord(p)
+        outer_pot[p - 1] = look_up(table + STEP * (zs * zs), to_level(level)) + dist
     for p in (0, slots - 1):
         put_field(w, (p,), (zero, zero), 0, True, end)
 
@@ -360,38 +308,34 @@
         cym = [get(coef, (i,), base) for i in (2, 3)]
         return c, linear(c, xp, xm, yp, ym, zp, zm, cyp, cym, cx)
 
-    def wait_plane(p, with_level):
-        @pl.when(at.valid(p))
-        def _():
-            psi_copy(p).wait()
-
-        if with_level:
-            @pl.when(at.valid(p) & (p < slots - 1))
-            def _():
-                dis_copy(p).wait()
-
-    wait_plane(0, False)
-    wait_plane(1, True)
-
-    def one_tile(p, j, level_at, masked):
+    def fill(p, j):
+        for i in range(2):
+            value = psi[i, at.plane(p), (j - 1) * ROWS : j * ROWS, :]
+            put(w, (i, p), jnp.where(at.valid(p), value, 0.0), j * ROWS)
+
+    for p in range(2):
+        for j in range(1, tiles + 1):
+            fill(p, j)
+
+    def potential(p, j):
+        return get(pot, (p - 1,), (j - 1) * ROWS) if j else outer_pot[p - 1]
+
+    def one_tile(p, j, masked):
         base, outer = j * ROWS, j == 0
         c, lin = field_linear(w, p, base, outer)
-        level = d[p - 1, pl.ds(base - ROWS if j else rows, ROWS), :]
-        here = look_up(level_at, level) + get(dist, (), base)
-        slope = first_slope(c, lin, here)
+        slope = first_slope(c, lin, potential(p, j))
         if outer:
             slope = [jnp.where(row_ok, s, 0.0) for s in slope]
         if masked:
             slope = [jnp.where(at.valid(p), s, 0.0) for s in slope]
         put_field(k, (p - 1,), slope, base, outer, end)
         put_field(lw, (p - 1,), lin, base, False, end)
-        put(pot, (p - 1,), here, base)
 
     def two_tile(p, j, full):
         base, outer = j * ROWS, j == 0
         c, lin = field_linear(k, p - 1, base, outer)
         z, rest = second_stage(
-            tile_of(w, (p,), base), c, tile_of(lw, (p - 1,), base), lin, get(pot, (p - 1,), base), full and not outer
+            tile_of(w, (p,), base), c, tile_of(lw, (p - 1,), base), lin, potential(p, j), full and not outer
         )
         if outer:
             z = [jnp.where(row_ok, s, 0.0) for s in z]
@@ -410,11 +354,10 @@
             put(part, lead, get(part, lead, base - ROWS) + lin[i], base - ROWS)
 
     def planes(p, masked, two, three):
-        wait_plane(p + 1, True)
-        zp = at.zcoord(p)
-        level_at = table + STEP * (zp * zp)
+        for j in range(1, tiles + 1):
+            fill(p + 1, j)
         for j in range(tiles + 1):
-            one_tile(p, j, level_at, masked)
+            one_tile(p, j, masked)
             if two is not None:
                 two_tile(p - 1, j, two)
             if three and j:
@@ -559,14 +502,14 @@
     levels = lambda *shape: pltpu.VMEM(shape, jnp.int32)
     dma = lambda *shape: pltpu.SemaphoreType.DMA(shape)
 
-    def call(kernel, name, ins, outs, out_specs, scratches, flops, moved, *args):
+    def call(kernel, name, room, ins, outs, out_specs, scratches, flops, moved, *args):
         return pl.pallas_call(
             functools.partial(kernel, dims),
             out_shape=outs,
             in_specs=ins,
             out_specs=out_specs,
             scratch_shapes=scratches,
-            compiler_params=pltpu.CompilerParams(vmem_limit_bytes=52 * 1024 * 1024),
+            compiler_params=pltpu.CompilerParams(vmem_limit_bytes=room * 1024 * 1024),
             cost_estimate=pl.CostEstimate(flops=flops, bytes_accessed=moved, transcendentals=0),
             name=name,
         )(*args)
@@ -584,23 +527,23 @@
     cells = share * rows * cols
     block = 4 * slots * rows * cols
     first, second = call(
-        rows_kernel, "pack_rows", [hbm] * 2, [f32(slots - 2, ROWS, LANES)] * 2, [vmem] * 2,
-        [scratch(2, slots, 2, ROWS, LANES), levels(slots, 2, ROWS, LANES), dma(slots, 2), dma(slots, 2)],
+        rows_kernel, "pack_rows", 52, [hbm] * 2, [f32(slots - 2, ROWS, LANES)] * 2, [vmem] * 2,
+        [scratch(2, 2, slots - 2, ROWS, LANES), levels(2, slots - 2, ROWS, LANES), dma(2), dma(2)],
         cells // 16, block // 8, psi, disorder,
     )
     first = send(first, row_pairs(0))
     second = send(second, row_pairs(1))
 
     packed = call(
-        columns_kernel, "pack_columns", [hbm] * 2, [f32(3, rows, LANES)] * sides + [f32(rows, LANES)] * sides,
-        [vmem] * (2 * sides),
-        [scratch(2, slots, rows, cols), levels(slots, rows, cols), dma(slots), dma(slots)],
-        9 * cells, 3 * block, psi, disorder,
+        columns_kernel, "pack_columns", 24, [vmem] * 2,
+        [f32(slots - 2, rows, cols)] + [f32(3, rows, LANES)] * sides + [f32(rows, LANES)] * sides,
+        [vmem] * (1 + 2 * sides), [], 12 * cells, 3 * block, psi, disorder,
     )
-    own, message = packed[:sides], packed[sides:]
+    pot = packed[0]
+    own, message = packed[1 : 1 + sides], packed[1 + sides :]
 
     made = call(
-        corner_kernel, "pack_corners", [vmem] * (2 + sides), [f32(3, ROWS, LANES)] * sides + [f32(tall, LANES)] * sides,
+        corner_kernel, "pack_corners", 24, [vmem] * (2 + sides), [f32(3, ROWS, LANES)] * sides + [f32(tall, LANES)] * sides,
         [vmem] * (2 * sides), [], cells // 8, block // 16, first, second, *message,
     )
     outer, message = made[:sides], made[sides:]
@@ -613,23 +556,19 @@
 
     field = lambda depth: scratch(2, depth, tall + ROWS, LANES)
     part = call(
-        step_kernel, "step", [hbm] * 2 + [vmem] * 2, f32(2, share, rows, cols), vmem,
+        step_kernel, "step", 24, [vmem] * 4, f32(2, share, rows, cols), vmem,
         [
             field(slots),
-            levels(slots - 2, tall, LANES),
             field(slots - 2),
             field(slots - 2),
-            scratch(slots - 2, tall, LANES),
+            scratch(slots - 2, ROWS, LANES),
             field(slots - 4),
             scratch(4, tall, LANES),
-            scratch(tall, LANES),
-            dma(slots),
-            dma(slots),
         ],
-        300 * cells, 4 * block, psi, disorder, first, second,
+        300 * cells, 4 * block, psi, pot, first, second,
     )
     return call(
-        strip_kernel, "strips", [vmem] * (1 + 3 * sides), f32(2, share, rows, cols), hbm,
+        strip_kernel, "strips", 24, [vmem] * (1 + 3 * sides), f32(2, share, rows, cols), hbm,
         [
             scratch(2, share, rows, cols),
             field(sides),

time: 22 us -> 19.5 us (0.89)
  the two profiles are of different devices: /device:TPU:10 before, /device:TPU:18 now
where the time goes in v2:
time: 19.5 us; the launch traced here: 19.3 us
  Pallas kernels  12.4 us (64%)
  starting transfers between devices  5.09 us (26%)
  waiting for transfers between devices  1.76 us (9%)
    pallas_call x5, Pallas kernels, call(): pl.pallas_call(functools.partial(kernel, dims), out_shape=outs, in_specs=...  12.4 us
    ppermute x3, starting transfers between devices, send(): return lax.ppermute(value, ('px', 'py'), pairs)  5.09 us
    ppermute x3, waiting for transfers between devices, send(): return lax.ppermute(value, ('px', 'py'), pairs)  1.76 us
  transfers between devices with their start and end apart: 3, of which 1 were waited for; matrix products, arithmetic and copies ran while one was open for 0% of the time, Pallas kernels for 45%

profile of v2, /device:TPU:18, one launch (start us, length us, event | category | flops | bytes accessed | tf_op | source)
XLA Modules:
  0.0 19.3 jit_solution(17017427166295222551)
XLA Ops:
  0.0 0.0 copy-start
  0.0 0.0 copy-start.1
  0.0 1.2 %pack_rows.1 = (f32[12,8,128]{2,1,0:T(8,128)S(1)}, f32[12,8,128]{2,1,0:T(8,128)S(1)}) custom-call(f32[2,32,128,128]{3,2,1,0:T(8,128)} %psi.5, s32[32,128,128]{2,1,0:T(8,128)} %dis.3), custom_call_target="tpu_custom_call" | custom-call | flops 8192 | bytes 114688 | tf_op jit(solution)/shard_map/pack_rows/pallas_call | solution.py:506
  1.2 1.6 %collective-permute-start = (f32[12,8,128]{2,1,0:T(8,128)S(1)}, f32[12,8,128]{2,1,0:T(8,128)S(1)}, u32[]{:S(2)}, u32[]{:S(2)}) collective-permute-start(f32[12,8,128]{2,1,0:T(8,128)S(1)} %get-tuple-element.13), channel_id=1, source_target_pairs={{0,2},{2,0},{1,3},{3,1},{4,6},{6,4},{5,7},{7,5},{8,10},{10,8},{9,1... | collective-permute-start | bytes 147464 | tf_op jit(solution)/shard_map/ppermute | solution.py:518
  2.9 1.9 %collective-permute-start.1 = (f32[12,8,128]{2,1,0:T(8,128)S(1)}, f32[12,8,128]{2,1,0:T(8,128)S(1)}, u32[]{:S(2)}, u32[]{:S(2)}) collective-permute-start(f32[12,8,128]{2,1,0:T(8,128)S(1)} %get-tuple-element.14), channel_id=1, source_target_pairs={{2,4},{4,2},{3,5},{5,3},{10,12},{12,10},{11,13},{13,11},{18,20},{2... | collective-permute-start | bytes 147464 | tf_op jit(solution)/shard_map/ppermute | solution.py:518
  4.8 0.0 copy-done
  4.8 0.0 copy-done.1
  4.8 2.3 %pack_columns.1 = (f32[12,128,128]{2,1,0:T(8,128)S(1)}, f32[3,128,128]{2,1,0:T(8,128)S(1)}, f32[128,128]{1,0:T(8,128)S(1)}) custom-call(f32[2,32,128,128]{3,2,1,0:T(8,128)S(1)} %copy-done, s32[32,128,128]{2,1,0:T(8,128)S(1)} %copy-done.1), custom_call_target="tpu_custom_call" | custom-call | flops 1572864 | bytes 2752512 | tf_op jit(solution)/shard_map/pack_columns/pallas_call | solution.py:506
  7.1 0.0 collective-permute-done.first
  7.1 1.8 %collective-permute-done.1.second = f32[12,8,128]{2,1,0:T(8,128)S(1)} collective-permute-done((f32[12,8,128]{2,1,0:T(8,128)S(1)}, f32[12,8,128]{2,1,0:T(8,128)S(1)}, u32[]{:S(2)}, u32[]{:S(2)}) %collective-permute-start.1) | collective-permute-done | bytes 49184 | tf_op jit(solution)/shard_map/ppermute | solution.py:518
  8.8 0.2 pack_corners.1
  9.0 1.5 %collective-permute-start.2 = (f32[136,128]{1,0:T(8,128)S(1)}, f32[136,128]{1,0:T(8,128)S(1)}, u32[]{:S(2)}, u32[]{:S(2)}) collective-permute-start(f32[136,128]{1,0:T(8,128)S(1)} %get-tuple-element.18), channel_id=1, source_target_pairs={{0,1},{2,3},{4,5},{6,7},{1,0},{3,2},{5,4},{7,6},{8,9},{10,11},{12,... | collective-permute-start | bytes 208904 | tf_op jit(solution)/shard_map/ppermute | solution.py:518
  10.5 6.4 %step.1.part = f32[2,8,128,128]{3,2,1,0:T(8,128)S(1)} custom-call(f32[2,32,128,128]{3,2,1,0:T(8,128)S(1)} %copy-done, f32[12,128,128]{2,1,0:T(8,128)S(1)} %get-tuple-element.12.pot, f32[12,8,128]{2,1,0:T(8,128)S(1)} %collective-permute-done.first, f32[12,8,128]{2,1,0:T(8,128)S(1)} %collective-permute-done.1.second), custom_call_target="tpu_custom_call" | custom-call | flops 39321600 | bytes 3670016 | tf_op jit(solution)/shard_map/step/pallas_call | solution.py:506
  17.0 0.0 collective-permute-done.2.refs_2_
  17.0 2.4 %strips.1 = f32[2,8,128,128]{3,2,1,0:T(8,128)} custom-call(f32[2,8,128,128]{3,2,1,0:T(8,128)S(1)} %step.1.part, f32[3,128,128]{2,1,0:T(8,128)S(1)} %get-tuple-element.15.refs_0_, f32[3,8,128]{2,1,0:T(8,128)S(1)} %get-tuple-element.17.refs_1_, f32[136,128]{1,0:T(8,128)S(1)} %collective-permute-done.2.refs_2_), custom_call_target="tpu_custom_call" | custom-call | flops 3932160 | bytes 1835008 | tf_op jit(solution)/shard_map/strips/pallas_call | solution.py:506
Async XLA Ops:
  0.0 4.8 %copy-start = (f32[2,32,128,128]{3,2,1,0:T(8,128)S(1)}, f32[2,32,128,128]{3,2,1,0:T(8,128)}, u32[]{:S(2)}) copy-start(f32[2,32,128,128]{3,2,1,0:T(8,128)} %psi.5) | copy-start | bytes 12582916
  0.0 4.8 %copy-start.1 = (s32[32,128,128]{2,1,0:T(8,128)S(1)}, s32[32,128,128]{2,1,0:T(8,128)}, u32[]{:S(2)}) copy-start(s32[32,128,128]{2,1,0:T(8,128)} %dis.3) | copy-start | bytes 6291460
  1.2 5.9 %collective-permute-start = (f32[12,8,128]{2,1,0:T(8,128)S(1)}, f32[12,8,128]{2,1,0:T(8,128)S(1)}, u32[]{:S(2)}, u32[]{:S(2)}) collective-permute-start(f32[12,8,128]{2,1,0:T(8,128)S(1)} %get-tuple-element.13), channel_id=1, source_target_pairs={{0,2},{2,0},{1,3},{3,1},{4,6},{6,4},{5,7},{7,5},{8,10},{10,8},{9,1... | collective-permute-start | bytes 147464 | tf_op jit(solution)/shard_map/ppermute | solution.py:518
  2.9 6.0 %collective-permute-start.1 = (f32[12,8,128]{2,1,0:T(8,128)S(1)}, f32[12,8,128]{2,1,0:T(8,128)S(1)}, u32[]{:S(2)}, u32[]{:S(2)}) collective-permute-start(f32[12,8,128]{2,1,0:T(8,128)S(1)} %get-tuple-element.14), channel_id=1, source_target_pairs={{2,4},{4,2},{3,5},{5,3},{10,12},{12,10},{11,13},{13,11},{18,20},{2... | collective-permute-start | bytes 147464 | tf_op jit(solution)/shard_map/ppermute | solution.py:518
  9.0 8.0 %collective-permute-start.2 = (f32[136,128]{1,0:T(8,128)S(1)}, f32[136,128]{1,0:T(8,128)S(1)}, u32[]{:S(2)}, u32[]{:S(2)}) collective-permute-start(f32[136,128]{1,0:T(8,128)S(1)} %get-tuple-element.18), channel_id=1, source_target_pairs={{0,1},{2,3},{4,5},{6,7},{1,0},{3,2},{5,4},{7,6},{8,9},{10,11},{12,... | collective-permute-start | bytes 208904 | tf_op jit(solution)/shard_map/ppermute | solution.py:518

commit v3 on v2

--- a/solution.py
+++ b/solution.py
@@ -15,13 +15,12 @@
 
 ROOT_OUT = math.sqrt((3.0 + 2.0 * math.sqrt(1.2)) / 7.0)
 ROOT_IN = math.sqrt((3.0 - 2.0 * math.sqrt(1.2)) / 7.0)
-PAIRS = (
-    (0.25 * ROOT_OUT * ROOT_OUT, (18.0 - math.sqrt(30.0)) / 36.0),
-    (0.25 * ROOT_IN * ROOT_IN, (18.0 + math.sqrt(30.0)) / 36.0),
-)
-KAPPA = STEP * COUPLING
-HALF = 0.5 * STEP
+WEIGHT_OUT = (18.0 - math.sqrt(30.0)) / 36.0
+WEIGHT_IN = 1.0 - WEIGHT_OUT
+
+LAP = 0.5 * STEP
 SPIN = 0.5 * STEP * ROTATION
+KAPPA = 0.5 * STEP * COUPLING
 
 DEEP = 3
 WIDE = 3 * DEEP
@@ -48,7 +47,7 @@
     lane = iota(1)
     table = jnp.zeros((ROWS, LANES), F32)
     for level in range(LEVELS):
-        table = jnp.where(lane == level, F32(STEP * 1.5 * math.sin(2.3 * level + 0.4)), table)
+        table = jnp.where(lane == level, F32(0.75 * STEP * math.sin(2.3 * level + 0.4)), table)
     return table
 
 
@@ -60,8 +59,12 @@
     return jnp.clip(value, 0.0, LEVELS - 1.0).astype(jnp.int32)
 
 
-def linear(c, xp, xm, yp, ym, zp, zm, cyp, cym, cx):
-    diag = [HALF * (zp[i] + zm[i]) - (6.0 * HALF) * c[i] for i in range(2)]
+def factors(spin, lap, scale):
+    return scale * (spin + lap), scale * (spin - lap)
+
+
+def linear(c, xp, xm, yp, ym, zp, zm, cyp, cym, cx, lap, lap_z):
+    diag = [lap_z * (zp[i] + zm[i]) - (6.0 * lap) * c[i] for i in range(2)]
     real = cyp[1] * yp[0] - cym[0] * ym[0] - cx[0] * xp[0] + cx[1] * xm[0] - diag[0]
     imag = cyp[0] * yp[1] - cym[1] * ym[1] - cx[1] * xp[1] + cx[0] * xm[1] + diag[1]
     return real, imag
@@ -73,30 +76,33 @@
 
 
 def second_stage(w, k, lin_w, lin_k, pot, full):
-    m = [w[i] + 0.5 * k[i] for i in range(2)]
+    m = [w[i] + k[i] for i in range(2)]
     p0 = pot + KAPPA * (m[0] * m[0] + m[1] * m[1])
     p1 = (2.0 * KAPPA) * (m[0] * k[0] + m[1] * k[1])
     p2 = KAPPA * (k[0] * k[0] + k[1] * k[1])
-    n0 = [p0 * m[i] for i in range(2)]
-    n1 = [p0 * k[i] + p1 * m[i] for i in range(2)]
-    n2 = [p1 * k[i] + p2 * m[i] for i in range(2)]
-    n3 = [p2 * k[i] for i in range(2)]
-    turn = lambda n: (n[1], -n[0])
-    f0 = [lin_w[i] + 0.5 * lin_k[i] + turn(n0)[i] for i in range(2)]
-    f1 = [lin_k[i] + turn(n1)[i] for i in range(2)]
-    f2 = turn(n2)
-    f3 = turn(n3)
-    base = [w[i] + 0.5 * f0[i] + (1.0 / 24.0) * f2[i] for i in range(2)]
-    z = [base[i] - (1.0 / 12.0) * f1[i] - (1.0 / 80.0) * f3[i] for i in range(2)]
+    f0 = lin_w[0] + lin_k[0] + p0 * m[1], lin_w[1] + lin_k[1] - p0 * m[0]
+    f1 = lin_k[0] + (p0 * k[1] + p1 * m[1]), lin_k[1] - (p0 * k[0] + p1 * m[0])
+    f2 = p1 * k[1] + p2 * m[1], p1 * k[0] + p2 * m[0]
+    f3 = p2 * k[1], p2 * k[0]
+    sign = 1.0, -1.0
+    base = [w[i] + f0[i] + (sign[i] / 3.0) * f2[i] for i in range(2)]
+    z = [base[i] - (1.0 / 3.0) * f1[i] - (sign[i] / 5.0) * f3[i] for i in range(2)]
     if not full:
         return z, None
-    total = [pot * z[i] for i in range(2)]
-    for sq, weight in PAIRS:
-        even = [base[i] + (0.5 * sq - 0.125) * f1[i] + (0.25 * sq * sq - 1.0 / 64.0) * f3[i] for i in range(2)]
-        odd = [f0[i] + (sq / 3.0) * f2[i] for i in range(2)]
-        scale = weight * KAPPA
-        p = scale * (even[0] * even[0] + even[1] * even[1]) + (scale * sq) * (odd[0] * odd[0] + odd[1] * odd[1])
-        q = (2.0 * scale * sq) * (even[0] * odd[0] + even[1] * odd[1])
+    square = ROOT_OUT * ROOT_OUT
+    even_out = [
+        base[i] + (0.5 * (square - 1.0)) * f1[i] + (sign[i] * 0.25 * (square * square - 1.0)) * f3[i] for i in range(2)
+    ]
+    even_in = [z[i] + (WEIGHT_OUT / WEIGHT_IN) * (z[i] - even_out[i]) for i in range(2)]
+    total = [(pot + pot) * z[i] for i in range(2)]
+    for even, square, weight in (
+        (even_out, ROOT_OUT * ROOT_OUT, WEIGHT_OUT),
+        (even_in, ROOT_IN * ROOT_IN, WEIGHT_IN),
+    ):
+        odd = [f0[i] + (sign[i] * square / 3.0) * f2[i] for i in range(2)]
+        scale = 2.0 * KAPPA * weight
+        p = scale * (even[0] * even[0] + even[1] * even[1]) + (scale * square) * (odd[0] * odd[0] + odd[1] * odd[1])
+        q = (2.0 * scale * square) * (even[0] * odd[0] + even[1] * odd[1])
         total = [total[i] + p * even[i] + q * odd[i] for i in range(2)]
     return z, (w[0] + total[1], w[1] - total[0])
 
@@ -185,11 +191,11 @@
     table = level_table()
     ys = at.ycoord(iota(1))
     here = [slot == jnp.where(at.valid(p), p, -1) for p in range(at.slots)]
-    level_at = [table + STEP * (at.zcoord(p) * at.zcoord(p)) for p in range(at.slots)]
+    level_at = [table + (0.5 * STEP) * (at.zcoord(p) * at.zcoord(p)) for p in range(at.slots)]
     for j in range(at.tiles):
         rows = slice(j * ROWS, (j + 1) * ROWS)
         xs = at.xcoord(sub + j * ROWS)
-        dist = STEP * (xs * xs + ys * ys)
+        dist = (0.5 * STEP) * (xs * xs + ys * ys)
         for p in range(1, at.slots - 1):
             pot[p - 1, rows, :] = look_up(level_at[p], dis[at.plane(p), rows, :]) + dist
         for side in range(at.sides):
@@ -275,43 +281,49 @@
     row_ok = (global_row >= 0) & (global_row < rows * at.npx)
 
     ys = at.ycoord(lane)
-    cx = (SPIN * ys + HALF, SPIN * ys - HALF)
+    cx = [factors(SPIN * ys, LAP, scale) for scale in (0.5, 1.0)]
     has_next = jnp.where(lane < cols - 1, 1.0, 0.0)
     has_prev = jnp.where(lane > 0, 1.0, 0.0)
     for j in range(tiles + 1):
         xs = at.xcoord(outer_row if j == 0 else sub + (j - 1) * ROWS)
         here = slice(j * ROWS, (j + 1) * ROWS)
-        coef[0, here] = (SPIN * xs + HALF) * has_next
-        coef[1, here] = (SPIN * xs - HALF) * has_next
-        coef[2, here] = (SPIN * xs + HALF) * has_prev
-        coef[3, here] = (SPIN * xs - HALF) * has_prev
+        for which, scale in enumerate((0.5, 1.0)):
+            for i, factor in enumerate(factors(SPIN * xs, LAP, scale)):
+                coef[4 * which + i, here] = factor * has_next
+                coef[4 * which + 2 + i, here] = factor * has_prev
 
     zero = jnp.zeros((ROWS, LANES), F32)
     xs = at.xcoord(outer_row)
-    dist = STEP * (xs * xs + ys * ys)
+    dist = (0.5 * STEP) * (xs * xs + ys * ys)
     for p in range(1, slots - 1):
         a, b, level = unpack_rows(sub, even, first[p - 1], second[p - 1])
         put_field(w, (p,), (a, b), 0, True, end)
         zs = at.zcoord(p)
-        outer_pot[p - 1] = look_up(table + STEP * (zs * zs), to_level(level)) + dist
+        outer_pot[p - 1] = look_up(table + (0.5 * STEP) * (zs * zs), to_level(level)) + dist
     for p in (0, slots - 1):
         put_field(w, (p,), (zero, zero), 0, True, end)
 
-    def field_linear(ref, q, base, outer):
+    def field_linear(ref, q, base, outer, lap_z, which=0):
         c = tile_of(ref, (q,), base)
         xp, xm = x_pair(ref, (q,), base, outer, end)
         zp = tile_of(ref, (q + 1,), base)
         zm = tile_of(ref, (q - 1,), base)
         yp = [roll(c[i], -1, 1) for i in range(2)]
         ym = [roll(c[i], 1, 1) for i in range(2)]
-        cyp = [get(coef, (i,), base) for i in (0, 1)]
-        cym = [get(coef, (i,), base) for i in (2, 3)]
-        return c, linear(c, xp, xm, yp, ym, zp, zm, cyp, cym, cx)
+        cyp = [get(coef, (4 * which + i,), base) for i in (0, 1)]
+        cym = [get(coef, (4 * which + i,), base) for i in (2, 3)]
+        lap = (0.5, 1.0)[which] * LAP
+        return c, linear(c, xp, xm, yp, ym, zp, zm, cyp, cym, cx[which], lap, lap if lap_z is None else lap_z)
+
+    for p in (*range(DEEP), *range(slots - DEEP, slots)):
+        @pl.when(jnp.logical_not(at.valid(p)))
+        def _():
+            w[:, p, ROWS:end] = jnp.zeros((2, rows, LANES), F32)
 
     def fill(p, j):
+        to = jnp.where(at.valid(p), p, slots)
         for i in range(2):
-            value = psi[i, at.plane(p), (j - 1) * ROWS : j * ROWS, :]
-            put(w, (i, p), jnp.where(at.valid(p), value, 0.0), j * ROWS)
+            put(w, (i, to), psi[i, at.plane(p), (j - 1) * ROWS : j * ROWS, :], j * ROWS)
 
     for p in range(2):
         for j in range(1, tiles + 1):
@@ -320,27 +332,23 @@
     def potential(p, j):
         return get(pot, (p - 1,), (j - 1) * ROWS) if j else outer_pot[p - 1]
 
-    def one_tile(p, j, masked):
+    def one_tile(p, j, lap_z):
         base, outer = j * ROWS, j == 0
-        c, lin = field_linear(w, p, base, outer)
+        c, lin = field_linear(w, p, base, outer, lap_z)
         slope = first_slope(c, lin, potential(p, j))
         if outer:
             slope = [jnp.where(row_ok, s, 0.0) for s in slope]
-        if masked:
-            slope = [jnp.where(at.valid(p), s, 0.0) for s in slope]
         put_field(k, (p - 1,), slope, base, outer, end)
         put_field(lw, (p - 1,), lin, base, False, end)
 
-    def two_tile(p, j, full):
+    def two_tile(p, j, full, lap_z):
         base, outer = j * ROWS, j == 0
-        c, lin = field_linear(k, p - 1, base, outer)
+        c, lin = field_linear(k, p - 1, base, outer, lap_z)
         z, rest = second_stage(
             tile_of(w, (p,), base), c, tile_of(lw, (p - 1,), base), lin, potential(p, j), full and not outer
         )
         if outer:
             z = [jnp.where(row_ok, s, 0.0) for s in z]
-        if not full:
-            z = [jnp.where(at.valid(p), s, 0.0) for s in z]
         put_field(zf, (p - 2,), z, base, outer, end)
         if rest is not None:
             for i in range(2):
@@ -348,34 +356,26 @@
 
     def three_tile(p, j):
         base = j * ROWS
-        _, lin = field_linear(zf, p - 2, base, False)
+        _, lin = field_linear(zf, p - 2, base, False, None, 1)
         for i in range(2):
             lead = (i, p - DEEP)
             put(part, lead, get(part, lead, base - ROWS) + lin[i], base - ROWS)
 
-    def planes(p, masked, two, three):
+    def planes(p, two, three):
+        lap_p = jnp.where(at.valid(p), 0.5 * LAP, 0.0)
+        lap_before = None if two else jnp.where(at.valid(p - 1), 0.5 * LAP, 0.0)
         for j in range(1, tiles + 1):
             fill(p + 1, j)
         for j in range(tiles + 1):
-            one_tile(p, j, masked)
+            one_tile(p, j, lap_p)
             if two is not None:
-                two_tile(p - 1, j, two)
+                two_tile(p - 1, j, two, lap_before)
             if three and j:
                 three_tile(p - 2, j)
 
-    def loop(start, stop, *what):
-        def body(p, carry):
-            planes(p, *what)
-            return carry
-
-        lax.fori_loop(start, stop, body, 0)
-
     last = slots - 2
-    loop(1, DEEP, True, None, False)
-    planes(jnp.int32(DEEP), False, False, False)
-    planes(jnp.int32(DEEP + 1), False, True, False)
-    loop(DEEP + 2, last, True, True, True)
-    planes(jnp.int32(last), True, False, True)
+    for p in range(1, last + 1):
+        planes(p, None if p < DEEP else p not in (DEEP, last), p > DEEP + 1)
 
 
 def strip_kernel(dims, part, *refs):
@@ -396,16 +396,16 @@
     for j in range(tiles + 1):
         xs = at.xcoord(outer_row if j == 0 else sub + (j - 1) * ROWS)
         here = slice(j * ROWS, (j + 1) * ROWS)
-        coef[0, here] = SPIN * xs + HALF
-        coef[1, here] = SPIN * xs - HALF
-        coef[2, here] = STEP * (xs * xs)
+        coef[0, here], coef[1, here] = factors(SPIN * xs, LAP, 0.5)
+        coef[2, here], coef[3, here] = factors(SPIN * xs, LAP, 1.0)
+        coef[4, here] = (0.5 * STEP) * (xs * xs)
 
     for side in range(at.sides):
         col = off + at.pick(side, -DEEP, cols - 2 * DEEP)
         ok = inside(at.z0 + slot, at.planes) & inside(at.py * cols + col, cols * at.npy)
         ys = at.ycoord(col)
-        cx = (SPIN * ys + HALF, SPIN * ys - HALF)
-        far = STEP * (zs * zs + ys * ys)
+        cx = factors(SPIN * ys, LAP, 0.5)
+        far = (0.5 * STEP) * (zs * zs + ys * ys)
         halo = at.pick(side, off, 8 - off) < DEEP
         back_b = at.pick(side, LANES - DEEP, DEEP)
         back_d = at.pick(side, LANES - 2 * DEEP, 2 * DEEP)
@@ -422,14 +422,14 @@
             b = jnp.where(halo, roll(new, back_b, 1), mine[1])
             level = to_level(jnp.where(halo, roll(new, back_d, 1), mine[2]))
             put_field(sw, (side,), (a, b), base, outer, end)
-            put(sp, (side,), look_up(table, level) + (far + get(coef, (2,), base)), base)
+            put(sp, (side,), look_up(table, level) + (far + get(coef, (4,), base)), base)
 
         def strip_linear(ref, base, outer):
             c = tile_of(ref, (side,), base)
             xp, xm = x_pair(ref, (side,), base, outer, end)
             yp, ym, zp, zm = [[roll(c[i], s, 1) for i in range(2)] for s in (-1, 1, -WIDE, WIDE)]
             cy = [get(coef, (i,), base) for i in (0, 1)]
-            return c, linear(c, xp, xm, yp, ym, zp, zm, cy, cy, cx)
+            return c, linear(c, xp, xm, yp, ym, zp, zm, cy, cy, cx, 0.5 * LAP, 0.5 * LAP)
 
         def keep(values, outer):
             good = (ok & row_ok) if outer else ok
@@ -459,17 +459,17 @@
 
     for side in range(at.sides):
         ys = at.ycoord(off + at.pick(side, -DEEP, cols - 2 * DEEP))
-        cx = (SPIN * ys + HALF, SPIN * ys - HALF)
+        cx = factors(SPIN * ys, LAP, 1.0)
         for j in range(1, tiles + 1):
             base = j * ROWS
             c = tile_of(sz, (side,), base)
             xp, xm = x_pair(sz, (side,), base, False, end)
             yp, ym, zp, zm = [[roll(c[i], s, 1) for i in range(2)] for s in (-1, 1, -WIDE, WIDE)]
-            cy = [get(coef, (i,), base) for i in (0, 1)]
-            lin = linear(c, xp, xm, yp, ym, zp, zm, cy, cy, cx)
+            cy = [get(coef, (i,), base) for i in (2, 3)]
+            lin = linear(c, xp, xm, yp, ym, zp, zm, cy, cy, cx, LAP, LAP)
             put_field(sk, (side,), [get(sl, (i, side), base) + lin[i] for i in range(2)], base, False, end)
 
-    def finish(p, carry):
+    for p in range(at.share):
         from_lane = DEEP + WIDE * (p + DEEP)
         for j in range(tiles):
             for i in range(2):
@@ -480,9 +480,6 @@
                     value = jnp.where(face, roll(get(sk, (i, side), (j + 1) * ROWS), shift, 1), value)
                 put(result, (i, p), value, j * ROWS)
         out_copy(p).start()
-        return carry
-
-    lax.fori_loop(0, at.share, finish, 0)
     for p in range(at.share):
         out_copy(p).wait()
 
@@ -558,12 +555,12 @@
     part = call(
         step_kernel, "step", 24, [vmem] * 4, f32(2, share, rows, cols), vmem,
         [
-            field(slots),
+            field(slots + 1),
             field(slots - 2),
             field(slots - 2),
             scratch(slots - 2, ROWS, LANES),
             field(slots - 4),
-            scratch(4, tall, LANES),
+            scratch(8, tall, LANES),
         ],
         300 * cells, 4 * block, psi, pot, first, second,
     )
@@ -576,7 +573,7 @@
             field(sides),
             scratch(sides, tall, LANES),
             field(sides),
-            scratch(3, tall, LANES),
+            scratch(5, tall, LANES),
             dma(share),
         ],
         30 * cells, 2 * block, part, *own, *outer, *got,

time: 19.5 us -> 17.3 us (0.89)
  the two profiles are of different devices: /device:TPU:18 before, /device:TPU:16 now
where the time goes in v3:
time: 17.3 us; the launch traced here: 17.1 us
  Pallas kernels  10.2 us (59%)
  starting transfers between devices  5.09 us (29%)
  waiting for transfers between devices  1.76 us (10%)
    pallas_call x5, Pallas kernels, call(): pl.pallas_call(functools.partial(kernel, dims), out_shape=outs, in_specs=...  10.2 us
    ppermute x3, starting transfers between devices, send(): return lax.ppermute(value, ('px', 'py'), pairs)  5.09 us
    ppermute x3, waiting for transfers between devices, send(): return lax.ppermute(value, ('px', 'py'), pairs)  1.76 us
  transfers between devices with their start and end apart: 3, of which 1 were waited for; matrix products, arithmetic and copies ran while one was open for 0% of the time, Pallas kernels for 41%

profile of v3, /device:TPU:16, one launch (start us, length us, event | category | flops | bytes accessed | tf_op | source)
XLA Modules:
  0.0 17.1 jit_solution(15389541253123407438)
XLA Ops:
  0.0 0.0 copy-start
  0.0 0.0 copy-start.1
  0.0 1.2 %pack_rows.1 = (f32[12,8,128]{2,1,0:T(8,128)S(1)}, f32[12,8,128]{2,1,0:T(8,128)S(1)}) custom-call(f32[2,32,128,128]{3,2,1,0:T(8,128)} %psi.5, s32[32,128,128]{2,1,0:T(8,128)} %dis.3), custom_call_target="tpu_custom_call" | custom-call | flops 8192 | bytes 114688 | tf_op jit(solution)/shard_map/pack_rows/pallas_call | solution.py:503
  1.2 1.6 %collective-permute-start = (f32[12,8,128]{2,1,0:T(8,128)S(1)}, f32[12,8,128]{2,1,0:T(8,128)S(1)}, u32[]{:S(2)}, u32[]{:S(2)}) collective-permute-start(f32[12,8,128]{2,1,0:T(8,128)S(1)} %get-tuple-element.13), channel_id=1, source_target_pairs={{0,2},{2,0},{1,3},{3,1},{4,6},{6,4},{5,7},{7,5},{8,10},{10,8},{9,1... | collective-permute-start | bytes 147464 | tf_op jit(solution)/shard_map/ppermute | solution.py:515
  2.9 1.9 %collective-permute-start.1 = (f32[12,8,128]{2,1,0:T(8,128)S(1)}, f32[12,8,128]{2,1,0:T(8,128)S(1)}, u32[]{:S(2)}, u32[]{:S(2)}) collective-permute-start(f32[12,8,128]{2,1,0:T(8,128)S(1)} %get-tuple-element.14), channel_id=1, source_target_pairs={{2,4},{4,2},{3,5},{5,3},{10,12},{12,10},{11,13},{13,11},{18,20},{2... | collective-permute-start | bytes 147464 | tf_op jit(solution)/shard_map/ppermute | solution.py:515
  4.8 0.0 copy-done
  4.8 0.0 copy-done.1
  4.8 2.3 %pack_columns.1 = (f32[12,128,128]{2,1,0:T(8,128)S(1)}, f32[3,128,128]{2,1,0:T(8,128)S(1)}, f32[128,128]{1,0:T(8,128)S(1)}) custom-call(f32[2,32,128,128]{3,2,1,0:T(8,128)S(1)} %copy-done, s32[32,128,128]{2,1,0:T(8,128)S(1)} %copy-done.1), custom_call_target="tpu_custom_call" | custom-call | flops 1572864 | bytes 2752512 | tf_op jit(solution)/shard_map/pack_columns/pallas_call | solution.py:503
  7.1 0.0 collective-permute-done.first
  7.1 1.8 %collective-permute-done.1.second = f32[12,8,128]{2,1,0:T(8,128)S(1)} collective-permute-done((f32[12,8,128]{2,1,0:T(8,128)S(1)}, f32[12,8,128]{2,1,0:T(8,128)S(1)}, u32[]{:S(2)}, u32[]{:S(2)}) %collective-permute-start.1) | collective-permute-done | bytes 49184 | tf_op jit(solution)/shard_map/ppermute | solution.py:515
  8.8 0.2 pack_corners.1
  9.0 1.5 %collective-permute-start.2 = (f32[136,128]{1,0:T(8,128)S(1)}, f32[136,128]{1,0:T(8,128)S(1)}, u32[]{:S(2)}, u32[]{:S(2)}) collective-permute-start(f32[136,128]{1,0:T(8,128)S(1)} %get-tuple-element.18), channel_id=1, source_target_pairs={{0,1},{2,3},{4,5},{6,7},{1,0},{3,2},{5,4},{7,6},{8,9},{10,11},{12,... | collective-permute-start | bytes 208904 | tf_op jit(solution)/shard_map/ppermute | solution.py:515
  10.5 4.7 %step.1.part = f32[2,8,128,128]{3,2,1,0:T(8,128)S(1)} custom-call(f32[2,32,128,128]{3,2,1,0:T(8,128)S(1)} %copy-done, f32[12,128,128]{2,1,0:T(8,128)S(1)} %get-tuple-element.12.pot, f32[12,8,128]{2,1,0:T(8,128)S(1)} %collective-permute-done.first, f32[12,8,128]{2,1,0:T(8,128)S(1)} %collective-permute-done.1.second), custom_call_target="tpu_custom_call" | custom-call | flops 39321600 | bytes 3670016 | tf_op jit(solution)/shard_map/step/pallas_call | solution.py:503
  15.3 0.0 collective-permute-done.2.refs_2_
  15.3 1.8 %strips.1 = f32[2,8,128,128]{3,2,1,0:T(8,128)} custom-call(f32[2,8,128,128]{3,2,1,0:T(8,128)S(1)} %step.1.part, f32[3,128,128]{2,1,0:T(8,128)S(1)} %get-tuple-element.15.refs_0_, f32[3,8,128]{2,1,0:T(8,128)S(1)} %get-tuple-element.17.refs_1_, f32[136,128]{1,0:T(8,128)S(1)} %collective-permute-done.2.refs_2_), custom_call_target="tpu_custom_call" | custom-call | flops 3932160 | bytes 1835008 | tf_op jit(solution)/shard_map/strips/pallas_call | solution.py:503
Async XLA Ops:
  0.0 4.8 %copy-start = (f32[2,32,128,128]{3,2,1,0:T(8,128)S(1)}, f32[2,32,128,128]{3,2,1,0:T(8,128)}, u32[]{:S(2)}) copy-start(f32[2,32,128,128]{3,2,1,0:T(8,128)} %psi.5) | copy-start | bytes 12582916
  0.0 4.8 %copy-start.1 = (s32[32,128,128]{2,1,0:T(8,128)S(1)}, s32[32,128,128]{2,1,0:T(8,128)}, u32[]{:S(2)}) copy-start(s32[32,128,128]{2,1,0:T(8,128)} %dis.3) | copy-start | bytes 6291460
  1.2 5.9 %collective-permute-start = (f32[12,8,128]{2,1,0:T(8,128)S(1)}, f32[12,8,128]{2,1,0:T(8,128)S(1)}, u32[]{:S(2)}, u32[]{:S(2)}) collective-permute-start(f32[12,8,128]{2,1,0:T(8,128)S(1)} %get-tuple-element.13), channel_id=1, source_target_pairs={{0,2},{2,0},{1,3},{3,1},{4,6},{6,4},{5,7},{7,5},{8,10},{10,8},{9,1... | collective-permute-start | bytes 147464 | tf_op jit(solution)/shard_map/ppermute | solution.py:515
  2.9 6.0 %collective-permute-start.1 = (f32[12,8,128]{2,1,0:T(8,128)S(1)}, f32[12,8,128]{2,1,0:T(8,128)S(1)}, u32[]{:S(2)}, u32[]{:S(2)}) collective-permute-start(f32[12,8,128]{2,1,0:T(8,128)S(1)} %get-tuple-element.14), channel_id=1, source_target_pairs={{2,4},{4,2},{3,5},{5,3},{10,12},{12,10},{11,13},{13,11},{18,20},{2... | collective-permute-start | bytes 147464 | tf_op jit(solution)/shard_map/ppermute | solution.py:515
  9.0 6.3 %collective-permute-start.2 = (f32[136,128]{1,0:T(8,128)S(1)}, f32[136,128]{1,0:T(8,128)S(1)}, u32[]{:S(2)}, u32[]{:S(2)}) collective-permute-start(f32[136,128]{1,0:T(8,128)S(1)} %get-tuple-element.18), channel_id=1, source_target_pairs={{0,1},{2,3},{4,5},{6,7},{1,0},{3,2},{5,4},{7,6},{8,9},{10,11},{12,... | collective-permute-start | bytes 208904 | tf_op jit(solution)/shard_map/ppermute | solution.py:515

commit v4 on v3

--- a/solution.py
+++ b/solution.py
@@ -117,9 +117,19 @@
         self.z0 = lax.axis_index("section") * self.share - DEEP
         self.px = lax.axis_index("px")
         self.py = lax.axis_index("py")
+        self.core = lax.axis_index("section") % 2
+        self.sends_up = (self.px + self.core) % 2 == 0
+        self.pair_planes = 2 * self.share + 2 * DEEP - 2
 
     def valid(self, p):
         return (self.z0 + p >= 0) & (self.z0 + p < self.planes)
+
+    def outer_row(self, sub):
+        return jnp.where(sub >= 4, sub - ROWS, self.rows + sub)
+
+    def on_grid(self, row):
+        row = self.px * self.rows + row
+        return (row >= 0) & (row < self.rows * self.npx)
 
     def plane(self, p):
         return jnp.clip(self.z0 + p, 0, self.planes - 1)
@@ -145,42 +155,44 @@
         return self.coordinate(self.z0 + slot, self.planes)
 
 
-def unpack_rows(sub, even, first, second):
-    up = jnp.where(even, second, first)
-    dn = jnp.where(even, first, second)
+def unpack_rows(at, p, got, other):
+    sub = iota(0)
+    index = p - 1 + at.core * at.share
+    got, other = got[index], other[index]
+    up = jnp.where(at.sends_up, other, got)
+    dn = jnp.where(at.sends_up, got, other)
     upper = sub >= 4
-    a = jnp.where(upper, up, dn)
-    b = jnp.where(upper, roll(up, 3, 0), roll(dn, -3, 0))
+    ok = at.on_grid(at.outer_row(sub))
+    a = jnp.where(ok, jnp.where(upper, up, dn), 0.0)
+    b = jnp.where(ok, jnp.where(upper, roll(up, 3, 0), roll(dn, -3, 0)), 0.0)
     level = jnp.where(upper, roll(up, -2, 0), roll(dn, 2, 0))
     return a, b, level
 
 
-def rows_kernel(dims, psi, dis, first, second, vpsi, vdis, psem, dsem):
+def rows_kernel(dims, psi, dis, message, vpsi, vdis, psem, dsem):
     at = Place(dims)
-    count = at.slots - 2
-    start = at.z0 + 1
-    window = jnp.clip(start, 0, at.planes - count)
-    span = pl.ds(window, count)
-    copies = []
-    for e, edge in enumerate((pl.ds(0, ROWS), pl.ds(at.rows - ROWS, ROWS))):
-        copies.append(pltpu.make_async_copy(psi.at[:, span, edge], vpsi.at[e], psem.at[e]))
-        copies.append(pltpu.make_async_copy(dis.at[span, edge], vdis.at[e], dsem.at[e]))
+    start = at.z0 - at.core * at.share + 1
+    window = jnp.clip(start, 0, at.planes - at.pair_planes)
+    edge = pl.ds(pl.multiple_of(jnp.where(at.sends_up, at.rows - ROWS, 0), ROWS), ROWS)
+    span = pl.ds(window, at.pair_planes)
+    copies = [
+        pltpu.make_async_copy(psi.at[:, span, edge], vpsi, psem),
+        pltpu.make_async_copy(dis.at[span, edge], vdis, dsem),
+    ]
     for copy in copies:
         copy.start()
     sub = iota(0)
-    even = at.px % 2 == 0
+    place = jnp.where(at.sends_up, ROWS - 1 - sub, sub)
+    shift_b = jnp.where(at.sends_up, ROWS - 3, 3)
+    shift_d = jnp.where(at.sends_up, 2, ROWS - 2)
     for copy in copies:
         copy.wait()
-    for t in range(count):
+    for t in range(at.pair_planes):
         z = start + t
-        index = jnp.clip(z - window, 0, count - 1)
-        inside = (z >= 0) & (z < at.planes)
-        a, b = [[vpsi[e, i, index] for e in range(2)] for i in range(2)]
-        level = [vdis[e, index].astype(F32) for e in range(2)]
-        up = jnp.where(sub >= 5, a[1], jnp.where(sub >= 2, roll(b[1], -3, 0), roll(level[1], 2, 0)))
-        dn = jnp.where(sub < 3, a[0], jnp.where(sub < 6, roll(b[0], 3, 0), roll(level[0], -2, 0)))
-        first[t] = jnp.where(inside, jnp.where(even, up, dn), 0.0)
-        second[t] = jnp.where(inside, jnp.where(even, dn, up), 0.0)
+        index = jnp.clip(z - window, 0, at.pair_planes - 1)
+        a, b, level = vpsi[0, index], vpsi[1, index], vdis[index].astype(F32)
+        value = jnp.where(place < 3, a, jnp.where(place < 6, roll(b, shift_b, 0), roll(level, shift_d, 0)))
+        message[t] = jnp.where((z >= 0) & (z < at.planes), value, 0.0)
 
 
 def columns_kernel(dims, psi, dis, pot, *refs):
@@ -221,14 +233,12 @@
     return jnp.where(place < DEEP, a, jnp.where(place < 2 * DEEP, b, level))
 
 
-def corner_kernel(dims, first, second, *refs):
+def corner_kernel(dims, got, other, *refs):
     at = Place(dims)
     message = refs[: at.sides]
     outer, whole = refs[at.sides : 2 * at.sides], refs[2 * at.sides :]
-    sub = iota(0)
-    even = at.px % 2 == 0
     slot, off = strip_lanes()
-    tiles = [unpack_rows(sub, even, first[p - 1], second[p - 1]) for p in range(1, at.slots - 1)]
+    tiles = [unpack_rows(at, p, got, other) for p in range(1, at.slots - 1)]
     for side in range(at.sides):
         shift = at.pick(side, DEEP, LANES - at.cols + 2 * DEEP)
         back = at.pick(side, DEEP, LANES - DEEP)
@@ -268,87 +278,104 @@
             put(ref, (i,) + lead, values[i], end)
 
 
-def step_kernel(dims, psi, pot, first, second, part, w, k, lw, outer_pot, zf, coef):
+class Stages:
+    def __init__(self, at, w, k, lw, coef, scales):
+        self.at, self.w, self.k, self.lw, self.coef = at, w, k, lw, coef
+        self.end = ROWS + at.rows
+        sub, lane = iota(0), iota(1)
+        self.outer_row = at.outer_row(sub)
+        self.row_ok = at.on_grid(self.outer_row)
+        self.ys = at.ycoord(lane)
+        self.cx = [factors(SPIN * self.ys, LAP, scale) for scale in scales]
+        self.scales = scales
+        has_next = jnp.where(lane < at.cols - 1, 1.0, 0.0)
+        has_prev = jnp.where(lane > 0, 1.0, 0.0)
+        for j in range(at.tiles + 1):
+            xs = at.xcoord(self.outer_row if j == 0 else sub + (j - 1) * ROWS)
+            here = slice(j * ROWS, (j + 1) * ROWS)
+            for which, scale in enumerate(scales):
+                for i, factor in enumerate(factors(SPIN * xs, LAP, scale)):
+                    coef[4 * which + i, here] = factor * has_next
+                    coef[4 * which + 2 + i, here] = factor * has_prev
+
+    def linear(self, ref, q, base, outer, lap_z, which=0):
+        c = tile_of(ref, (q,), base)
+        xp, xm = x_pair(ref, (q,), base, outer, self.end)
+        zp = tile_of(ref, (q + 1,), base)
+        zm = tile_of(ref, (q - 1,), base)
+        yp = [roll(c[i], -1, 1) for i in range(2)]
+        ym = [roll(c[i], 1, 1) for i in range(2)]
+        cyp = [get(self.coef, (4 * which + i,), base) for i in (0, 1)]
+        cym = [get(self.coef, (4 * which + i,), base) for i in (2, 3)]
+        lap = self.scales[which] * LAP
+        return c, linear(c, xp, xm, yp, ym, zp, zm, cyp, cym, self.cx[which], lap, lap if lap_z is None else lap_z)
+
+    def one(self, p, j, pot, lap_z):
+        base, outer = j * ROWS, j == 0
+        c, lin = self.linear(self.w, p, base, outer, lap_z)
+        slope = first_slope(c, lin, pot)
+        if outer:
+            slope = [jnp.where(self.row_ok, s, 0.0) for s in slope]
+        put_field(self.k, (p - 1,), slope, base, outer, self.end)
+        put_field(self.lw, (p - 1,), lin, base, False, self.end)
+
+    def lap_of(self, p):
+        return jnp.where(self.at.valid(p), self.scales[0] * LAP, 0.0)
+
+
+def slopes_kernel(dims, psi, pot, w, k, lw, coef):
     at = Place(dims)
-    slots, tiles, rows, cols = at.slots, at.tiles, at.rows, at.cols
-    end = ROWS + rows
-    sub = iota(0)
-    lane = iota(1)
+    stages = Stages(at, w, k, lw, coef, (0.5,))
+
+    for p in (*range(DEEP), *range(at.slots - DEEP, at.slots)):
+        @pl.when(jnp.logical_not(at.valid(p)))
+        def _():
+            w[:, p, ROWS : stages.end] = jnp.zeros((2, at.rows, LANES), F32)
+
+    def fill(p):
+        to = jnp.where(at.valid(p), p, at.slots)
+        for j in range(1, at.tiles + 1):
+            for i in range(2):
+                put(w, (i, to), psi[i, at.plane(p), (j - 1) * ROWS : j * ROWS, :], j * ROWS)
+
+    fill(0)
+    fill(1)
+    for p in range(1, at.slots - 1):
+        fill(p + 1)
+        lap_p = stages.lap_of(p)
+        for j in range(2, at.tiles):
+            stages.one(p, j, get(pot, (p - 1,), (j - 1) * ROWS), lap_p)
+
+
+def step_kernel(dims, pot, got, other, w_in, k_in, lw_in, part, w, k, lw, outer_pot, zf, coef):
+    at = Place(dims)
+    slots, tiles, rows = at.slots, at.tiles, at.rows
+    stages = Stages(at, w, k, lw, coef, (0.5, 1.0))
+    end, ys = stages.end, stages.ys
     table = level_table()
-    even = at.px % 2 == 0
-    outer_row = jnp.where(sub >= 4, sub - ROWS, rows + sub)
-    global_row = at.px * rows + outer_row
-    row_ok = (global_row >= 0) & (global_row < rows * at.npx)
-
-    ys = at.ycoord(lane)
-    cx = [factors(SPIN * ys, LAP, scale) for scale in (0.5, 1.0)]
-    has_next = jnp.where(lane < cols - 1, 1.0, 0.0)
-    has_prev = jnp.where(lane > 0, 1.0, 0.0)
-    for j in range(tiles + 1):
-        xs = at.xcoord(outer_row if j == 0 else sub + (j - 1) * ROWS)
-        here = slice(j * ROWS, (j + 1) * ROWS)
-        for which, scale in enumerate((0.5, 1.0)):
-            for i, factor in enumerate(factors(SPIN * xs, LAP, scale)):
-                coef[4 * which + i, here] = factor * has_next
-                coef[4 * which + 2 + i, here] = factor * has_prev
 
     zero = jnp.zeros((ROWS, LANES), F32)
-    xs = at.xcoord(outer_row)
+    xs = at.xcoord(stages.outer_row)
     dist = (0.5 * STEP) * (xs * xs + ys * ys)
     for p in range(1, slots - 1):
-        a, b, level = unpack_rows(sub, even, first[p - 1], second[p - 1])
+        a, b, level = unpack_rows(at, p, got, other)
         put_field(w, (p,), (a, b), 0, True, end)
         zs = at.zcoord(p)
         outer_pot[p - 1] = look_up(table + (0.5 * STEP) * (zs * zs), to_level(level)) + dist
     for p in (0, slots - 1):
         put_field(w, (p,), (zero, zero), 0, True, end)
 
-    def field_linear(ref, q, base, outer, lap_z, which=0):
-        c = tile_of(ref, (q,), base)
-        xp, xm = x_pair(ref, (q,), base, outer, end)
-        zp = tile_of(ref, (q + 1,), base)
-        zm = tile_of(ref, (q - 1,), base)
-        yp = [roll(c[i], -1, 1) for i in range(2)]
-        ym = [roll(c[i], 1, 1) for i in range(2)]
-        cyp = [get(coef, (4 * which + i,), base) for i in (0, 1)]
-        cym = [get(coef, (4 * which + i,), base) for i in (2, 3)]
-        lap = (0.5, 1.0)[which] * LAP
-        return c, linear(c, xp, xm, yp, ym, zp, zm, cyp, cym, cx[which], lap, lap if lap_z is None else lap_z)
-
-    for p in (*range(DEEP), *range(slots - DEEP, slots)):
-        @pl.when(jnp.logical_not(at.valid(p)))
-        def _():
-            w[:, p, ROWS:end] = jnp.zeros((2, rows, LANES), F32)
-
-    def fill(p, j):
-        to = jnp.where(at.valid(p), p, slots)
-        for i in range(2):
-            put(w, (i, to), psi[i, at.plane(p), (j - 1) * ROWS : j * ROWS, :], j * ROWS)
-
-    for p in range(2):
-        for j in range(1, tiles + 1):
-            fill(p, j)
-
     def potential(p, j):
         return get(pot, (p - 1,), (j - 1) * ROWS) if j else outer_pot[p - 1]
 
-    def one_tile(p, j, lap_z):
-        base, outer = j * ROWS, j == 0
-        c, lin = field_linear(w, p, base, outer, lap_z)
-        slope = first_slope(c, lin, potential(p, j))
-        if outer:
-            slope = [jnp.where(row_ok, s, 0.0) for s in slope]
-        put_field(k, (p - 1,), slope, base, outer, end)
-        put_field(lw, (p - 1,), lin, base, False, end)
-
     def two_tile(p, j, full, lap_z):
         base, outer = j * ROWS, j == 0
-        c, lin = field_linear(k, p - 1, base, outer, lap_z)
+        c, lin = stages.linear(k, p - 1, base, outer, lap_z)
         z, rest = second_stage(
             tile_of(w, (p,), base), c, tile_of(lw, (p - 1,), base), lin, potential(p, j), full and not outer
         )
         if outer:
-            z = [jnp.where(row_ok, s, 0.0) for s in z]
+            z = [jnp.where(stages.row_ok, s, 0.0) for s in z]
         put_field(zf, (p - 2,), z, base, outer, end)
         if rest is not None:
             for i in range(2):
@@ -356,26 +383,23 @@
 
     def three_tile(p, j):
         base = j * ROWS
-        _, lin = field_linear(zf, p - 2, base, False, None, 1)
+        _, lin = stages.linear(zf, p - 2, base, False, None, 1)
         for i in range(2):
             lead = (i, p - DEEP)
             put(part, lead, get(part, lead, base - ROWS) + lin[i], base - ROWS)
 
-    def planes(p, two, three):
-        lap_p = jnp.where(at.valid(p), 0.5 * LAP, 0.0)
-        lap_before = None if two else jnp.where(at.valid(p - 1), 0.5 * LAP, 0.0)
-        for j in range(1, tiles + 1):
-            fill(p + 1, j)
+    last = slots - 2
+    for p in range(1, last + 1):
+        two = None if p < DEEP else p not in (DEEP, last)
+        lap_p = stages.lap_of(p)
+        lap_before = None if two else stages.lap_of(p - 1)
         for j in range(tiles + 1):
-            one_tile(p, j, lap_p)
+            if j < 2 or j == tiles:
+                stages.one(p, j, potential(p, j), lap_p)
             if two is not None:
                 two_tile(p - 1, j, two, lap_before)
-            if three and j:
+            if p > DEEP + 1 and j:
                 three_tile(p - 2, j)
-
-    last = slots - 2
-    for p in range(1, last + 1):
-        planes(p, None if p < DEEP else p not in (DEEP, last), p > DEEP + 1)
 
 
 def strip_kernel(dims, part, *refs):
@@ -388,9 +412,9 @@
     lane = iota(1)
     slot, off = strip_lanes()
     table = level_table()
-    outer_row = jnp.where(sub >= 4, sub - ROWS, rows + sub)
+    outer_row = at.outer_row(sub)
     inside = lambda index, count: (index >= 0) & (index < count)
-    row_ok = inside(at.px * rows + outer_row, rows * at.npx)
+    row_ok = at.on_grid(outer_row)
     zs = at.zcoord(slot)
 
     for j in range(tiles + 1):
@@ -499,13 +523,14 @@
     levels = lambda *shape: pltpu.VMEM(shape, jnp.int32)
     dma = lambda *shape: pltpu.SemaphoreType.DMA(shape)
 
-    def call(kernel, name, room, ins, outs, out_specs, scratches, flops, moved, *args):
+    def call(kernel, name, room, ins, outs, out_specs, scratches, flops, moved, *args, aliases={}):
         return pl.pallas_call(
             functools.partial(kernel, dims),
             out_shape=outs,
             in_specs=ins,
             out_specs=out_specs,
             scratch_shapes=scratches,
+            input_output_aliases=aliases,
             compiler_params=pltpu.CompilerParams(vmem_limit_bytes=room * 1024 * 1024),
             cost_estimate=pl.CostEstimate(flops=flops, bytes_accessed=moved, transcendentals=0),
             name=name,
@@ -514,34 +539,47 @@
     def send(value, pairs):
         return lax.ppermute(value, ("px", "py"), pairs)
 
-    def row_pairs(start):
-        found = []
-        for i in range(start, npx - 1, 2):
+    sections = lax.axis_size("section")
+    place = lambda s, i, j: (s * npx + i) * npy + j
+    row_pairs = []
+    for s in range(sections):
+        for i in range(npx):
+            partner = i ^ 1 if s % 2 == 0 else ((i + 1) ^ 1) - 1
             for j in range(npy):
-                found += [(i * npy + j, (i + 1) * npy + j), ((i + 1) * npy + j, i * npy + j)]
-        return found
+                to = (partner, j) if 0 <= partner < npx else (i, j ^ 1)
+                if to[1] < npy:
+                    row_pairs.append((place(s, i, j), place(s, *to)))
+    core_pairs = [(s, s ^ 1) for s in range(sections)]
 
     cells = share * rows * cols
     block = 4 * slots * rows * cols
-    first, second = call(
-        rows_kernel, "pack_rows", 52, [hbm] * 2, [f32(slots - 2, ROWS, LANES)] * 2, [vmem] * 2,
-        [scratch(2, 2, slots - 2, ROWS, LANES), levels(2, slots - 2, ROWS, LANES), dma(2), dma(2)],
+    pair_planes = 2 * share + 2 * DEEP - 2
+    edges = call(
+        rows_kernel, "pack_rows", 52, [hbm] * 2, f32(pair_planes, ROWS, LANES), vmem,
+        [scratch(2, pair_planes, ROWS, LANES), levels(pair_planes, ROWS, LANES), dma(), dma()],
         cells // 16, block // 8, psi, disorder,
     )
-    first = send(first, row_pairs(0))
-    second = send(second, row_pairs(1))
+    edges = lax.ppermute(edges, ("section", "px", "py"), row_pairs)
 
     packed = call(
         columns_kernel, "pack_columns", 24, [vmem] * 2,
         [f32(slots - 2, rows, cols)] + [f32(3, rows, LANES)] * sides + [f32(rows, LANES)] * sides,
         [vmem] * (1 + 2 * sides), [], 12 * cells, 3 * block, psi, disorder,
     )
+    edges, packed = lax.optimization_barrier((edges, packed))
     pot = packed[0]
     own, message = packed[1 : 1 + sides], packed[1 + sides :]
+    others = lax.ppermute(edges, "section", core_pairs)
+    field = lambda depth: (2, depth, tall + ROWS, LANES)
+    begun = call(
+        slopes_kernel, "slopes", 24, [vmem] * 2, [f32(*field(n)) for n in (slots + 1, slots - 2, slots - 2)], [vmem] * 3,
+        [scratch(4, tall, LANES)], 60 * cells, 4 * block, psi, pot,
+    )
+    others, begun = lax.optimization_barrier((others, begun))
 
     made = call(
         corner_kernel, "pack_corners", 24, [vmem] * (2 + sides), [f32(3, ROWS, LANES)] * sides + [f32(tall, LANES)] * sides,
-        [vmem] * (2 * sides), [], cells // 8, block // 16, first, second, *message,
+        [vmem] * (2 * sides), [], cells // 8, block // 16, edges, others, *message,
     )
     outer, message = made[:sides], made[sides:]
     right = [(i * npy + j, i * npy + j + 1) for i in range(npx) for j in range(npy - 1)]
@@ -551,28 +589,21 @@
     else:
         got = [send(message[1], right), send(message[0], left)]
 
-    field = lambda depth: scratch(2, depth, tall + ROWS, LANES)
     part = call(
-        step_kernel, "step", 24, [vmem] * 4, f32(2, share, rows, cols), vmem,
-        [
-            field(slots + 1),
-            field(slots - 2),
-            field(slots - 2),
-            scratch(slots - 2, ROWS, LANES),
-            field(slots - 4),
-            scratch(8, tall, LANES),
-        ],
-        300 * cells, 4 * block, psi, pot, first, second,
-    )
+        step_kernel, "step", 24, [vmem] * 6,
+        [f32(2, share, rows, cols)] + [f32(*field(n)) for n in (slots + 1, slots - 2, slots - 2)], [vmem] * 4,
+        [scratch(slots - 2, ROWS, LANES), scratch(*field(slots - 4)), scratch(8, tall, LANES)],
+        240 * cells, 4 * block, pot, edges, others, *begun, aliases={3: 1, 4: 2, 5: 3},
+    )[0]
     return call(
         strip_kernel, "strips", 24, [vmem] * (1 + 3 * sides), f32(2, share, rows, cols), hbm,
         [
             scratch(2, share, rows, cols),
-            field(sides),
-            field(sides),
-            field(sides),
+            scratch(*field(sides)),
+            scratch(*field(sides)),
+            scratch(*field(sides)),
             scratch(sides, tall, LANES),
-            field(sides),
+            scratch(*field(sides)),
             scratch(5, tall, LANES),
             dma(share),
         ],

time: 17.3 us -> 16.1 us (0.931)
  the two profiles are of different devices: /device:TPU:16 before, /device:TPU:0 now
where the time goes in v4:
time: 16.1 us; the launch traced here: 16 us
  Pallas kernels  10.7 us (66%)
  starting transfers between devices  5.09 us (32%)
    pallas_call x6, Pallas kernels, call(): pl.pallas_call(functools.partial(kernel, dims), out_shape=outs, in_specs=...  10.7 us
    ppermute x1, starting transfers between devices, local(): edges = lax.ppermute(edges, ('section', 'px', 'py'), row_pairs)  3.1 us
    ppermute x1, starting transfers between devices, send(): return lax.ppermute(value, ('px', 'py'), pairs)  1.98 us
  transfers between devices with their start and end apart: 3, of which 1 were waited for; matrix products, arithmetic and copies ran while one was open for 0% of the time, Pallas kernels for 47%

profile of v4, /device:TPU:0, one launch (start us, length us, event | category | flops | bytes accessed | tf_op | source)
XLA Modules:
  0.0 16.0 jit_solution(14363763460982237749)
XLA Ops:
  0.0 0.0 copy-start
  0.0 0.0 copy-start.1
  0.0 1.2 %pack_rows.1 = f32[20,8,128]{2,1,0:T(8,128)S(1)} custom-call(f32[2,32,128,128]{3,2,1,0:T(8,128)} %psi.5, s32[32,128,128]{2,1,0:T(8,128)} %dis.3), custom_call_target="tpu_custom_call" | custom-call | flops 8192 | bytes 114688 | tf_op jit(solution)/shard_map/pack_rows/pallas_call | solution.py:527
  1.2 3.1 %collective-permute-start = (f32[20,8,128]{2,1,0:T(8,128)S(1)}, f32[20,8,128]{2,1,0:T(8,128)S(1)}, u32[]{:S(2)}, u32[]{:S(2)}) collective-permute-start(f32[20,8,128]{2,1,0:T(8,128)S(1)} %pack_rows.1), channel_id=1, source_target_pairs={{0,2},{1,3},{2,0},{3,1},{4,6},{5,7},{6,4},{7,5},{8,9},{9,8},{10,12... | collective-permute-start | bytes 245768 | tf_op jit(solution)/shard_map/ppermute | solution.py:562
  4.3 0.0 copy-done
  4.3 0.0 copy-done.1
  4.3 2.3 %pack_columns.1 = (f32[12,128,128]{2,1,0:T(8,128)S(1)}, f32[3,128,128]{2,1,0:T(8,128)S(1)}, f32[128,128]{1,0:T(8,128)S(1)}) custom-call(f32[2,32,128,128]{3,2,1,0:T(8,128)S(1)} %copy-done, s32[32,128,128]{2,1,0:T(8,128)S(1)} %copy-done.1), custom_call_target="tpu_custom_call" | custom-call | flops 1572864 | bytes 2752512 | tf_op jit(solution)/shard_map/pack_columns/pallas_call | solution.py:527
  6.6 0.1 collective-permute-done.got
  6.8 0.0 collective-permute-start.1
  6.8 1.4 %slopes.1 = (f32[2,15,144,128]{3,2,1,0:T(8,128)S(1)}, f32[2,12,144,128]{3,2,1,0:T(8,128)S(1)}, f32[2,12,144,128]{3,2,1,0:T(8,128)S(1)}) custom-call(f32[2,32,128,128]{3,2,1,0:T(8,128)S(1)} %copy-done, f32[12,128,128]{2,1,0:T(8,128)S(1)} %get-tuple-element.25.pot), custom_call_target="tpu_custom_call" | custom-call | flops 7864320 | bytes 3670016 | tf_op jit(solution)/shard_map/slopes/pallas_call | solution.py:527
  8.2 0.0 collective-permute-done.1.other
  8.2 0.2 %pack_corners.1 = (f32[3,8,128]{2,1,0:T(8,128)S(1)}, f32[136,128]{1,0:T(8,128)S(1)}) custom-call(f32[20,8,128]{2,1,0:T(8,128)S(1)} %collective-permute-done.got, f32[20,8,128]{2,1,0:T(8,128)S(1)} %collective-permute-done.1.other, f32[128,128]{1,0:T(8,128)S(1)} %get-tuple-element.36.refs_0_), custom_call_target="tpu_custom_call" | custom-call | flops 16384 | bytes 57344 | tf_op jit(solution)/shard_map/pack_corners/pallas_call | solution.py:527
  8.4 2.0 %collective-permute-start.2 = (f32[136,128]{1,0:T(8,128)S(1)}, f32[136,128]{1,0:T(8,128)S(1)}, u32[]{:S(2)}, u32[]{:S(2)}) collective-permute-start(f32[136,128]{1,0:T(8,128)S(1)} %get-tuple-element.38), channel_id=1, source_target_pairs={{0,1},{2,3},{4,5},{6,7},{1,0},{3,2},{5,4},{7,6},{8,9},{10,11},{12,... | collective-permute-start | bytes 208904 | tf_op jit(solution)/shard_map/ppermute | solution.py:540
  10.3 3.8 %step.1 = (f32[2,8,128,128]{3,2,1,0:T(8,128)S(1)}, f32[2,15,144,128]{3,2,1,0:T(8,128)S(1)}, f32[2,12,144,128]{3,2,1,0:T(8,128)S(1)}, f32[2,12,144,128]{3,2,1,0:T(8,128)S(1)}) custom-call(f32[12,128,128]{2,1,0:T(8,128)S(1)} %get-tuple-element.25.pot, ...), custom_call_target="tpu_custom_call", output_to_operand_aliasing={{1}: (3, {}), {2}: (4, {}), {3}: (5, {})} | custom-call | flops 31457280 | bytes 3670016 | tf_op jit(solution)/shard_map/step/pallas_call | solution.py:527
  14.2 0.0 collective-permute-done.2.refs_2_
  14.2 1.8 %strips.1 = f32[2,8,128,128]{3,2,1,0:T(8,128)} custom-call(f32[2,8,128,128]{3,2,1,0:T(8,128)S(1)} %get-tuple-element.34.part, f32[3,128,128]{2,1,0:T(8,128)S(1)} %get-tuple-element.35.refs_0_, f32[3,8,128]{2,1,0:T(8,128)S(1)} %get-tuple-element.37.refs_1_, f32[136,128]{1,0:T(8,128)S(1)} %collective-permute-done.2.refs_2_), custom_call_target="tpu_custom_call" | custom-call | flops 3932160 | bytes 1835008 | tf_op jit(solution)/shard_map/strips/pallas_call | solution.py:527
Async XLA Ops:
  0.0 4.3 %copy-start = (f32[2,32,128,128]{3,2,1,0:T(8,128)S(1)}, f32[2,32,128,128]{3,2,1,0:T(8,128)}, u32[]{:S(2)}) copy-start(f32[2,32,128,128]{3,2,1,0:T(8,128)} %psi.5) | copy-start | bytes 12582916
  0.0 4.3 %copy-start.1 = (s32[32,128,128]{2,1,0:T(8,128)S(1)}, s32[32,128,128]{2,1,0:T(8,128)}, u32[]{:S(2)}) copy-start(s32[32,128,128]{2,1,0:T(8,128)} %dis.3) | copy-start | bytes 6291460
  1.2 5.5 %collective-permute-start = (f32[20,8,128]{2,1,0:T(8,128)S(1)}, f32[20,8,128]{2,1,0:T(8,128)S(1)}, u32[]{:S(2)}, u32[]{:S(2)}) collective-permute-start(f32[20,8,128]{2,1,0:T(8,128)S(1)} %pack_rows.1), channel_id=1, source_target_pairs={{0,2},{1,3},{2,0},{3,1},{4,6},{5,7},{6,4},{7,5},{8,9},{9,8},{10,12... | collective-permute-start | bytes 245768 | tf_op jit(solution)/shard_map/ppermute | solution.py:562
  6.8 1.4 %collective-permute-start.1 = (f32[20,8,128]{2,1,0:T(8,128)S(1)}, f32[20,8,128]{2,1,0:T(8,128)S(1)}, u32[]{:S(2)}, u32[]{:S(2)}) collective-permute-start(f32[20,8,128]{2,1,0:T(8,128)S(1)} %collective-permute-done.got), channel_id=1, source_target_pairs={{0,8},{8,0},{16,24},{24,16},{1,9},{9,1},{17,25},{25,17},{2,10},{10... | collective-permute-start | bytes 245768 | tf_op jit(solution)/shard_map/ppermute | solution.py:572
  8.4 5.8 %collective-permute-start.2 = (f32[136,128]{1,0:T(8,128)S(1)}, f32[136,128]{1,0:T(8,128)S(1)}, u32[]{:S(2)}, u32[]{:S(2)}) collective-permute-start(f32[136,128]{1,0:T(8,128)S(1)} %get-tuple-element.38), channel_id=1, source_target_pairs={{0,1},{2,3},{4,5},{6,7},{1,0},{3,2},{5,4},{7,6},{8,9},{10,11},{12,... | collective-permute-start | bytes 208904 | tf_op jit(solution)/shard_map/ppermute | solution.py:540

commit v5 on v4

--- a/solution.py
+++ b/solution.py
@@ -26,6 +26,7 @@
 WIDE = 3 * DEEP
 LANES = 128
 ROWS = 8
+AHEAD = 6
 F32 = jnp.float32
 
 
@@ -75,15 +76,27 @@
     return lin[0] + g * w[1], lin[1] - g * w[0]
 
 
-def second_stage(w, k, lin_w, lin_k, pot, full):
+def powers(w, k, lin_w, pot):
     m = [w[i] + k[i] for i in range(2)]
     p0 = pot + KAPPA * (m[0] * m[0] + m[1] * m[1])
     p1 = (2.0 * KAPPA) * (m[0] * k[0] + m[1] * k[1])
     p2 = KAPPA * (k[0] * k[0] + k[1] * k[1])
-    f0 = lin_w[0] + lin_k[0] + p0 * m[1], lin_w[1] + lin_k[1] - p0 * m[0]
-    f1 = lin_k[0] + (p0 * k[1] + p1 * m[1]), lin_k[1] - (p0 * k[0] + p1 * m[0])
-    f2 = p1 * k[1] + p2 * m[1], p1 * k[0] + p2 * m[0]
-    f3 = p2 * k[1], p2 * k[0]
+    return (
+        lin_w[0] + p0 * m[1],
+        lin_w[1] - p0 * m[0],
+        p0 * k[1] + p1 * m[1],
+        -(p0 * k[0] + p1 * m[0]),
+        p1 * k[1] + p2 * m[1],
+        p1 * k[0] + p2 * m[0],
+        p2 * k[1],
+        p2 * k[0],
+    )
+
+
+def second_stage(w, parts, lin_k, pot, full):
+    f0 = parts[0] + lin_k[0], parts[1] + lin_k[1]
+    f1 = parts[2] + lin_k[0], parts[3] + lin_k[1]
+    f2, f3 = parts[4:6], parts[6:8]
     sign = 1.0, -1.0
     base = [w[i] + f0[i] + (sign[i] / 3.0) * f2[i] for i in range(2)]
     z = [base[i] - (1.0 / 3.0) * f1[i] - (sign[i] / 5.0) * f3[i] for i in range(2)]
@@ -318,25 +331,22 @@
             slope = [jnp.where(self.row_ok, s, 0.0) for s in slope]
         put_field(self.k, (p - 1,), slope, base, outer, self.end)
         put_field(self.lw, (p - 1,), lin, base, False, self.end)
+        return c, slope, lin
 
     def lap_of(self, p):
         return jnp.where(self.at.valid(p), self.scales[0] * LAP, 0.0)
 
 
-def slopes_kernel(dims, psi, pot, w, k, lw, coef):
+def slopes_kernel(dims, psi, pot, w, k, lw, ready, coef):
     at = Place(dims)
     stages = Stages(at, w, k, lw, coef, (0.5,))
 
-    for p in (*range(DEEP), *range(at.slots - DEEP, at.slots)):
-        @pl.when(jnp.logical_not(at.valid(p)))
-        def _():
-            w[:, p, ROWS : stages.end] = jnp.zeros((2, at.rows, LANES), F32)
-
     def fill(p):
-        to = jnp.where(at.valid(p), p, at.slots)
+        sure = DEEP <= p < at.slots - DEEP
         for j in range(1, at.tiles + 1):
             for i in range(2):
-                put(w, (i, to), psi[i, at.plane(p), (j - 1) * ROWS : j * ROWS, :], j * ROWS)
+                value = psi[i, at.plane(p), (j - 1) * ROWS : j * ROWS, :]
+                put(w, (i, p), value if sure else jnp.where(at.valid(p), value, 0.0), j * ROWS)
 
     fill(0)
     fill(1)
@@ -344,10 +354,14 @@
         fill(p + 1)
         lap_p = stages.lap_of(p)
         for j in range(2, at.tiles):
-            stages.one(p, j, get(pot, (p - 1,), (j - 1) * ROWS), lap_p)
-
-
-def step_kernel(dims, pot, got, other, w_in, k_in, lw_in, part, w, k, lw, outer_pot, zf, coef):
+            here = get(pot, (p - 1,), (j - 1) * ROWS)
+            values = stages.one(p, j, here, lap_p)
+            if DEEP <= p < DEEP + AHEAD:
+                for i, part in enumerate(powers(*values, here)):
+                    put(ready, (i, p - DEEP), part, (j - 2) * ROWS)
+
+
+def step_kernel(dims, pot, got, other, ready, w_in, k_in, lw_in, part, w, k, lw, outer_pot, zf, coef):
     at = Place(dims)
     slots, tiles, rows = at.slots, at.tiles, at.rows
     stages = Stages(at, w, k, lw, coef, (0.5, 1.0))
@@ -371,9 +385,12 @@
     def two_tile(p, j, full, lap_z):
         base, outer = j * ROWS, j == 0
         c, lin = stages.linear(k, p - 1, base, outer, lap_z)
-        z, rest = second_stage(
-            tile_of(w, (p,), base), c, tile_of(lw, (p - 1,), base), lin, potential(p, j), full and not outer
-        )
+        here, field = potential(p, j), tile_of(w, (p,), base)
+        if DEEP <= p < DEEP + AHEAD and 2 <= j < tiles:
+            parts = [get(ready, (i, p - DEEP), (j - 2) * ROWS) for i in range(8)]
+        else:
+            parts = powers(field, c, tile_of(lw, (p - 1,), base), here)
+        z, rest = second_stage(field, parts, lin, here, full and not outer)
         if outer:
             z = [jnp.where(stages.row_ok, s, 0.0) for s in z]
         put_field(zf, (p - 2,), z, base, outer, end)
@@ -467,9 +484,9 @@
 
         def strip_two(base, outer):
             c, lin = strip_linear(sk, base, outer)
-            z, rest = second_stage(
-                tile_of(sw, (side,), base), c, tile_of(sl, (side,), base), lin, get(sp, (side,), base), not outer
-            )
+            field, here = tile_of(sw, (side,), base), get(sp, (side,), base)
+            parts = powers(field, c, tile_of(sl, (side,), base), here)
+            z, rest = second_stage(field, parts, lin, here, not outer)
             put_field(sz, (side,), keep(z, outer), base, outer, end)
             if rest is not None:
                 put_field(sl, (side,), rest, base, False, end)
@@ -572,7 +589,8 @@
     others = lax.ppermute(edges, "section", core_pairs)
     field = lambda depth: (2, depth, tall + ROWS, LANES)
     begun = call(
-        slopes_kernel, "slopes", 24, [vmem] * 2, [f32(*field(n)) for n in (slots + 1, slots - 2, slots - 2)], [vmem] * 3,
+        slopes_kernel, "slopes", 24, [vmem] * 2,
+        [f32(*field(n)) for n in (slots, slots - 2, slots - 2)] + [f32(8, AHEAD, rows - 2 * ROWS, LANES)], [vmem] * 4,
         [scratch(4, tall, LANES)], 60 * cells, 4 * block, psi, pot,
     )
     others, begun = lax.optimization_barrier((others, begun))
@@ -590,10 +608,10 @@
         got = [send(message[1], right), send(message[0], left)]
 
     part = call(
-        step_kernel, "step", 24, [vmem] * 6,
-        [f32(2, share, rows, cols)] + [f32(*field(n)) for n in (slots + 1, slots - 2, slots - 2)], [vmem] * 4,
+        step_kernel, "step", 24, [vmem] * 7,
+        [f32(2, share, rows, cols)] + [f32(*field(n)) for n in (slots, slots - 2, slots - 2)], [vmem] * 4,
         [scratch(slots - 2, ROWS, LANES), scratch(*field(slots - 4)), scratch(8, tall, LANES)],
-        240 * cells, 4 * block, pot, edges, others, *begun, aliases={3: 1, 4: 2, 5: 3},
+        240 * cells, 4 * block, pot, edges, others, begun[3], *begun[:3], aliases={4: 1, 5: 2, 6: 3},
     )[0]
     return call(
         strip_kernel, "strips", 24, [vmem] * (1 + 3 * sides), f32(2, share, rows, cols), hbm,

time: 16.1 us -> 15.6 us (0.969)
  Pallas kernels: 10.7 us -> 10.2 us
    pallas_call x6, Pallas kernels: 10.7 us -> 10.2 us  [call(): pl.pallas_call(functools.partial(kernel, dims), out_shape=outs, in_specs=...]
  transfers between devices with their start and end apart: 3 -> 3, of which waited for: 1 -> 1; matrix products, arithmetic and copies ran while one was open for 0% -> 0% of each run, Pallas kernels for 47% -> 45%
where the time goes in v5:
time: 15.6 us; the launch traced here: 15.5 us
  Pallas kernels  10.2 us (65%)
  starting transfers between devices  5.09 us (33%)
    pallas_call x6, Pallas kernels, call(): pl.pallas_call(functools.partial(kernel, dims), out_shape=outs, in_specs=...  10.2 us
    ppermute x1, starting transfers between devices, local(): edges = lax.ppermute(edges, ('section', 'px', 'py'), row_pairs)  3.1 us
    ppermute x1, starting transfers between devices, send(): return lax.ppermute(value, ('px', 'py'), pairs)  1.98 us
  transfers between devices with their start and end apart: 3, of which 1 were waited for; matrix products, arithmetic and copies ran while one was open for 0% of the time, Pallas kernels for 45%

profile of v5, /device:TPU:0, one launch (start us, length us, event | category | flops | bytes accessed | tf_op | source)
XLA Modules:
  0.0 15.5 jit_solution(1083416558348468958)
XLA Ops:
  0.0 0.0 copy-start
  0.0 0.0 copy-start.1
  0.0 1.2 %pack_rows.1 = f32[20,8,128]{2,1,0:T(8,128)S(1)} custom-call(f32[2,32,128,128]{3,2,1,0:T(8,128)} %psi.5, s32[32,128,128]{2,1,0:T(8,128)} %dis.3), custom_call_target="tpu_custom_call" | custom-call | flops 8192 | bytes 114688 | tf_op jit(solution)/shard_map/pack_rows/pallas_call | solution.py:544
  1.2 3.1 %collective-permute-start = (f32[20,8,128]{2,1,0:T(8,128)S(1)}, f32[20,8,128]{2,1,0:T(8,128)S(1)}, u32[]{:S(2)}, u32[]{:S(2)}) collective-permute-start(f32[20,8,128]{2,1,0:T(8,128)S(1)} %pack_rows.1), channel_id=1, source_target_pairs={{0,2},{1,3},{2,0},{3,1},{4,6},{5,7},{6,4},{7,5},{8,9},{9,8},{10,12... | collective-permute-start | bytes 245768 | tf_op jit(solution)/shard_map/ppermute | solution.py:579
  4.3 0.0 copy-done
  4.3 0.0 copy-done.1
  4.3 2.3 %pack_columns.1 = (f32[12,128,128]{2,1,0:T(8,128)S(1)}, f32[3,128,128]{2,1,0:T(8,128)S(1)}, f32[128,128]{1,0:T(8,128)S(1)}) custom-call(f32[2,32,128,128]{3,2,1,0:T(8,128)S(1)} %copy-done, s32[32,128,128]{2,1,0:T(8,128)S(1)} %copy-done.1), custom_call_target="tpu_custom_call" | custom-call | flops 1572864 | bytes 2752512 | tf_op jit(solution)/shard_map/pack_columns/pallas_call | solution.py:544
  6.6 0.1 collective-permute-done.got
  6.8 0.0 collective-permute-start.1
  6.8 1.3 %slopes.1 = (f32[2,14,144,128]{3,2,1,0:T(8,128)S(1)}, f32[2,12,144,128]{3,2,1,0:T(8,128)S(1)}, f32[2,12,144,128]{3,2,1,0:T(8,128)S(1)}, f32[8,6,112,128]{3,2,1,0:T(8,128)S(1)}) custom-call(f32[2,32,128,128]{3,2,1,0:T(8,128)S(1)} %copy-done, f32[12,128,128]{2,1,0:T(8,128)S(1)} %get-tuple-element.27.pot), custom_call_target="tpu_custom_call" | custom-call | flops 7864320 | bytes 3670016 | tf_op jit(solution)/shard_map/slopes/pallas_call | solution.py:544
  8.1 0.0 collective-permute-done.1.other
  8.1 0.2 %pack_corners.1 = (f32[3,8,128]{2,1,0:T(8,128)S(1)}, f32[136,128]{1,0:T(8,128)S(1)}) custom-call(f32[20,8,128]{2,1,0:T(8,128)S(1)} %collective-permute-done.got, f32[20,8,128]{2,1,0:T(8,128)S(1)} %collective-permute-done.1.other, f32[128,128]{1,0:T(8,128)S(1)} %get-tuple-element.40.refs_0_), custom_call_target="tpu_custom_call" | custom-call | flops 16384 | bytes 57344 | tf_op jit(solution)/shard_map/pack_corners/pallas_call | solution.py:544
  8.3 2.0 %collective-permute-start.2 = (f32[136,128]{1,0:T(8,128)S(1)}, f32[136,128]{1,0:T(8,128)S(1)}, u32[]{:S(2)}, u32[]{:S(2)}) collective-permute-start(f32[136,128]{1,0:T(8,128)S(1)} %get-tuple-element.42), channel_id=1, source_target_pairs={{0,1},{2,3},{4,5},{6,7},{1,0},{3,2},{5,4},{7,6},{8,9},{10,11},{12,... | collective-permute-start | bytes 208904 | tf_op jit(solution)/shard_map/ppermute | solution.py:557
  10.2 3.4 %step.1 = (f32[2,8,128,128]{3,2,1,0:T(8,128)S(1)}, f32[2,14,144,128]{3,2,1,0:T(8,128)S(1)}, f32[2,12,144,128]{3,2,1,0:T(8,128)S(1)}, f32[2,12,144,128]{3,2,1,0:T(8,128)S(1)}) custom-call(f32[12,128,128]{2,1,0:T(8,128)S(1)} %get-tuple-element.27.pot, ...), custom_call_target="tpu_custom_call", output_to_operand_aliasing={{1}: (4, {}), {2}: (5, {}), {3}: (6, {})} | custom-call | flops 31457280 | bytes 3670016 | tf_op jit(solution)/shard_map/step/pallas_call | solution.py:544
  13.7 0.0 collective-permute-done.2.refs_2_
  13.7 1.8 %strips.1 = f32[2,8,128,128]{3,2,1,0:T(8,128)} custom-call(f32[2,8,128,128]{3,2,1,0:T(8,128)S(1)} %get-tuple-element.38.part, f32[3,128,128]{2,1,0:T(8,128)S(1)} %get-tuple-element.39.refs_0_, f32[3,8,128]{2,1,0:T(8,128)S(1)} %get-tuple-element.41.refs_1_, f32[136,128]{1,0:T(8,128)S(1)} %collective-permute-done.2.refs_2_), custom_call_target="tpu_custom_call" | custom-call | flops 3932160 | bytes 1835008 | tf_op jit(solution)/shard_map/strips/pallas_call | solution.py:544
Async XLA Ops:
  0.0 4.3 %copy-start = (f32[2,32,128,128]{3,2,1,0:T(8,128)S(1)}, f32[2,32,128,128]{3,2,1,0:T(8,128)}, u32[]{:S(2)}) copy-start(f32[2,32,128,128]{3,2,1,0:T(8,128)} %psi.5) | copy-start | bytes 12582916
  0.0 4.3 %copy-start.1 = (s32[32,128,128]{2,1,0:T(8,128)S(1)}, s32[32,128,128]{2,1,0:T(8,128)}, u32[]{:S(2)}) copy-start(s32[32,128,128]{2,1,0:T(8,128)} %dis.3) | copy-start | bytes 6291460
  1.2 5.5 %collective-permute-start = (f32[20,8,128]{2,1,0:T(8,128)S(1)}, f32[20,8,128]{2,1,0:T(8,128)S(1)}, u32[]{:S(2)}, u32[]{:S(2)}) collective-permute-start(f32[20,8,128]{2,1,0:T(8,128)S(1)} %pack_rows.1), channel_id=1, source_target_pairs={{0,2},{1,3},{2,0},{3,1},{4,6},{5,7},{6,4},{7,5},{8,9},{9,8},{10,12... | collective-permute-start | bytes 245768 | tf_op jit(solution)/shard_map/ppermute | solution.py:579
  6.8 1.3 %collective-permute-start.1 = (f32[20,8,128]{2,1,0:T(8,128)S(1)}, f32[20,8,128]{2,1,0:T(8,128)S(1)}, u32[]{:S(2)}, u32[]{:S(2)}) collective-permute-start(f32[20,8,128]{2,1,0:T(8,128)S(1)} %collective-permute-done.got), channel_id=1, source_target_pairs={{0,8},{8,0},{16,24},{24,16},{1,9},{9,1},{17,25},{25,17},{2,10},{10... | collective-permute-start | bytes 245768 | tf_op jit(solution)/shard_map/ppermute | solution.py:589
  8.3 5.4 %collective-permute-start.2 = (f32[136,128]{1,0:T(8,128)S(1)}, f32[136,128]{1,0:T(8,128)S(1)}, u32[]{:S(2)}, u32[]{:S(2)}) collective-permute-start(f32[136,128]{1,0:T(8,128)S(1)} %get-tuple-element.42), channel_id=1, source_target_pairs={{0,1},{2,3},{4,5},{6,7},{1,0},{3,2},{5,4},{7,6},{8,9},{10,11},{12,... | collective-permute-start | bytes 208904 | tf_op jit(solution)/shard_map/ppermute | solution.py:557

commit v6 on v5

--- a/solution.py
+++ b/solution.py
@@ -188,10 +188,13 @@
     window = jnp.clip(start, 0, at.planes - at.pair_planes)
     edge = pl.ds(pl.multiple_of(jnp.where(at.sends_up, at.rows - ROWS, 0), ROWS), ROWS)
     span = pl.ds(window, at.pair_planes)
-    copies = [
-        pltpu.make_async_copy(psi.at[:, span, edge], vpsi, psem),
-        pltpu.make_async_copy(dis.at[span, edge], vdis, dsem),
-    ]
+    copies = []
+    half = at.pair_planes // 2
+    for h in range(2):
+        span, to = pl.ds(window + h * half, half), pl.ds(h * half, half)
+        for i in range(2):
+            copies.append(pltpu.make_async_copy(psi.at[i, span, edge], vpsi.at[i, to], psem.at[h, i]))
+        copies.append(pltpu.make_async_copy(dis.at[span, edge], vdis.at[to], dsem.at[h]))
     for copy in copies:
         copy.start()
     sub = iota(0)
@@ -573,7 +576,7 @@
     pair_planes = 2 * share + 2 * DEEP - 2
     edges = call(
         rows_kernel, "pack_rows", 52, [hbm] * 2, f32(pair_planes, ROWS, LANES), vmem,
-        [scratch(2, pair_planes, ROWS, LANES), levels(pair_planes, ROWS, LANES), dma(), dma()],
+        [scratch(2, pair_planes, ROWS, LANES), levels(pair_planes, ROWS, LANES), dma(2, 2), dma(2)],
         cells // 16, block // 8, psi, disorder,
     )
     edges = lax.ppermute(edges, ("section", "px", "py"), row_pairs)

time: 15.6 us -> 15.6 us (level)
  no operation moved by 1% of the time
where the time goes in v6:
time: 15.6 us; the launch traced here: 15.4 us
  Pallas kernels  10.2 us (65%)
  starting transfers between devices  5.09 us (33%)
    pallas_call x6, Pallas kernels, call(): pl.pallas_call(functools.partial(kernel, dims), out_shape=outs, in_specs=...  10.2 us
    ppermute x1, starting transfers between devices, local(): edges = lax.ppermute(edges, ('section', 'px', 'py'), row_pairs)  3.1 us
    ppermute x1, starting transfers between devices, send(): return lax.ppermute(value, ('px', 'py'), pairs)  1.98 us
  transfers between devices with their start and end apart: 3, of which 1 were waited for; matrix products, arithmetic and copies ran while one was open for 0% of the time, Pallas kernels for 45%

profile of v6, /device:TPU:0, one launch (start us, length us, event | category | flops | bytes accessed | tf_op | source)
XLA Modules:
  0.0 15.4 jit_solution(9246998997427663591)
XLA Ops:
  0.0 0.0 copy-start
  0.0 0.0 copy-start.1
  0.0 1.2 %pack_rows.1 = f32[20,8,128]{2,1,0:T(8,128)S(1)} custom-call(f32[2,32,128,128]{3,2,1,0:T(8,128)} %psi.5, s32[32,128,128]{2,1,0:T(8,128)} %dis.3), custom_call_target="tpu_custom_call" | custom-call | flops 8192 | bytes 114688 | tf_op jit(solution)/shard_map/pack_rows/pallas_call | solution.py:547
  1.2 3.1 %collective-permute-start = (f32[20,8,128]{2,1,0:T(8,128)S(1)}, f32[20,8,128]{2,1,0:T(8,128)S(1)}, u32[]{:S(2)}, u32[]{:S(2)}) collective-permute-start(f32[20,8,128]{2,1,0:T(8,128)S(1)} %pack_rows.1), channel_id=1, source_target_pairs={{0,2},{1,3},{2,0},{3,1},{4,6},{5,7},{6,4},{7,5},{8,9},{9,8},{10,12... | collective-permute-start | bytes 245768 | tf_op jit(solution)/shard_map/ppermute | solution.py:582
  4.3 0.0 copy-done
  4.3 0.0 copy-done.1
  4.3 2.3 %pack_columns.1 = (f32[12,128,128]{2,1,0:T(8,128)S(1)}, f32[3,128,128]{2,1,0:T(8,128)S(1)}, f32[128,128]{1,0:T(8,128)S(1)}) custom-call(f32[2,32,128,128]{3,2,1,0:T(8,128)S(1)} %copy-done, s32[32,128,128]{2,1,0:T(8,128)S(1)} %copy-done.1), custom_call_target="tpu_custom_call" | custom-call | flops 1572864 | bytes 2752512 | tf_op jit(solution)/shard_map/pack_columns/pallas_call | solution.py:547
  6.6 0.1 collective-permute-done.got
  6.7 0.0 collective-permute-start.1
  6.7 1.3 %slopes.1 = (f32[2,14,144,128]{3,2,1,0:T(8,128)S(1)}, f32[2,12,144,128]{3,2,1,0:T(8,128)S(1)}, f32[2,12,144,128]{3,2,1,0:T(8,128)S(1)}, f32[8,6,112,128]{3,2,1,0:T(8,128)S(1)}) custom-call(f32[2,32,128,128]{3,2,1,0:T(8,128)S(1)} %copy-done, f32[12,128,128]{2,1,0:T(8,128)S(1)} %get-tuple-element.27.pot), custom_call_target="tpu_custom_call" | custom-call | flops 7864320 | bytes 3670016 | tf_op jit(solution)/shard_map/slopes/pallas_call | solution.py:547
  8.0 0.0 collective-permute-done.1.other
  8.0 0.2 %pack_corners.1 = (f32[3,8,128]{2,1,0:T(8,128)S(1)}, f32[136,128]{1,0:T(8,128)S(1)}) custom-call(f32[20,8,128]{2,1,0:T(8,128)S(1)} %collective-permute-done.got, f32[20,8,128]{2,1,0:T(8,128)S(1)} %collective-permute-done.1.other, f32[128,128]{1,0:T(8,128)S(1)} %get-tuple-element.40.refs_0_), custom_call_target="tpu_custom_call" | custom-call | flops 16384 | bytes 57344 | tf_op jit(solution)/shard_map/pack_corners/pallas_call | solution.py:547
  8.2 2.0 %collective-permute-start.2 = (f32[136,128]{1,0:T(8,128)S(1)}, f32[136,128]{1,0:T(8,128)S(1)}, u32[]{:S(2)}, u32[]{:S(2)}) collective-permute-start(f32[136,128]{1,0:T(8,128)S(1)} %get-tuple-element.42), channel_id=1, source_target_pairs={{0,1},{2,3},{4,5},{6,7},{1,0},{3,2},{5,4},{7,6},{8,9},{10,11},{12,... | collective-permute-start | bytes 208904 | tf_op jit(solution)/shard_map/ppermute | solution.py:560
  10.2 3.4 %step.1 = (f32[2,8,128,128]{3,2,1,0:T(8,128)S(1)}, f32[2,14,144,128]{3,2,1,0:T(8,128)S(1)}, f32[2,12,144,128]{3,2,1,0:T(8,128)S(1)}, f32[2,12,144,128]{3,2,1,0:T(8,128)S(1)}) custom-call(f32[12,128,128]{2,1,0:T(8,128)S(1)} %get-tuple-element.27.pot, ...), custom_call_target="tpu_custom_call", output_to_operand_aliasing={{1}: (4, {}), {2}: (5, {}), {3}: (6, {})} | custom-call | flops 31457280 | bytes 3670016 | tf_op jit(solution)/shard_map/step/pallas_call | solution.py:547
  13.6 0.0 collective-permute-done.2.refs_2_
  13.6 1.8 %strips.1 = f32[2,8,128,128]{3,2,1,0:T(8,128)} custom-call(f32[2,8,128,128]{3,2,1,0:T(8,128)S(1)} %get-tuple-element.38.part, f32[3,128,128]{2,1,0:T(8,128)S(1)} %get-tuple-element.39.refs_0_, f32[3,8,128]{2,1,0:T(8,128)S(1)} %get-tuple-element.41.refs_1_, f32[136,128]{1,0:T(8,128)S(1)} %collective-permute-done.2.refs_2_), custom_call_target="tpu_custom_call" | custom-call | flops 3932160 | bytes 1835008 | tf_op jit(solution)/shard_map/strips/pallas_call | solution.py:547
Async XLA Ops:
  0.0 4.3 %copy-start = (f32[2,32,128,128]{3,2,1,0:T(8,128)S(1)}, f32[2,32,128,128]{3,2,1,0:T(8,128)}, u32[]{:S(2)}) copy-start(f32[2,32,128,128]{3,2,1,0:T(8,128)} %psi.5) | copy-start | bytes 12582916
  0.0 4.3 %copy-start.1 = (s32[32,128,128]{2,1,0:T(8,128)S(1)}, s32[32,128,128]{2,1,0:T(8,128)}, u32[]{:S(2)}) copy-start(s32[32,128,128]{2,1,0:T(8,128)} %dis.3) | copy-start | bytes 6291460
  1.2 5.5 %collective-permute-start = (f32[20,8,128]{2,1,0:T(8,128)S(1)}, f32[20,8,128]{2,1,0:T(8,128)S(1)}, u32[]{:S(2)}, u32[]{:S(2)}) collective-permute-start(f32[20,8,128]{2,1,0:T(8,128)S(1)} %pack_rows.1), channel_id=1, source_target_pairs={{0,2},{1,3},{2,0},{3,1},{4,6},{5,7},{6,4},{7,5},{8,9},{9,8},{10,12... | collective-permute-start | bytes 245768 | tf_op jit(solution)/shard_map/ppermute | solution.py:582
  6.7 1.3 %collective-permute-start.1 = (f32[20,8,128]{2,1,0:T(8,128)S(1)}, f32[20,8,128]{2,1,0:T(8,128)S(1)}, u32[]{:S(2)}, u32[]{:S(2)}) collective-permute-start(f32[20,8,128]{2,1,0:T(8,128)S(1)} %collective-permute-done.got), channel_id=1, source_target_pairs={{0,8},{8,0},{16,24},{24,16},{1,9},{9,1},{17,25},{25,17},{2,10},{10... | collective-permute-start | bytes 245768 | tf_op jit(solution)/shard_map/ppermute | solution.py:592
  8.2 5.4 %collective-permute-start.2 = (f32[136,128]{1,0:T(8,128)S(1)}, f32[136,128]{1,0:T(8,128)S(1)}, u32[]{:S(2)}, u32[]{:S(2)}) collective-permute-start(f32[136,128]{1,0:T(8,128)S(1)} %get-tuple-element.42), channel_id=1, source_target_pairs={{0,1},{2,3},{4,5},{6,7},{1,0},{3,2},{5,4},{7,6},{8,9},{10,11},{12,... | collective-permute-start | bytes 208904 | tf_op jit(solution)/shard_map/ppermute | solution.py:560

commit v7 on v6

--- a/solution.py
+++ b/solution.py
@@ -85,7 +85,7 @@
         lin_w[0] + p0 * m[1],
         lin_w[1] - p0 * m[0],
         p0 * k[1] + p1 * m[1],
-        -(p0 * k[0] + p1 * m[0]),
+        p0 * k[0] + p1 * m[0],
         p1 * k[1] + p2 * m[1],
         p1 * k[0] + p2 * m[0],
         p2 * k[1],
@@ -95,7 +95,7 @@
 
 def second_stage(w, parts, lin_k, pot, full):
     f0 = parts[0] + lin_k[0], parts[1] + lin_k[1]
-    f1 = parts[2] + lin_k[0], parts[3] + lin_k[1]
+    f1 = lin_k[0] + parts[2], lin_k[1] - parts[3]
     f2, f3 = parts[4:6], parts[6:8]
     sign = 1.0, -1.0
     base = [w[i] + f0[i] + (sign[i] / 3.0) * f2[i] for i in range(2)]

time: 15.6 us -> 15.6 us (level)
  no operation moved by 1% of the time
where the time goes in v7:
time: 15.6 us; the launch traced here: 15.4 us
  Pallas kernels  10.1 us (65%)
  starting transfers between devices  5.09 us (33%)
    pallas_call x6, Pallas kernels, call(): pl.pallas_call(functools.partial(kernel, dims), out_shape=outs, in_specs=...  10.1 us
    ppermute x1, starting transfers between devices, local(): edges = lax.ppermute(edges, ('section', 'px', 'py'), row_pairs)  3.1 us
    ppermute x1, starting transfers between devices, send(): return lax.ppermute(value, ('px', 'py'), pairs)  1.98 us
  transfers between devices with their start and end apart: 3, of which 1 were waited for; matrix products, arithmetic and copies ran while one was open for 0% of the time, Pallas kernels for 45%

profile of v7, /device:TPU:0, one launch (start us, length us, event | category | flops | bytes accessed | tf_op | source)
XLA Modules:
  0.0 15.4 jit_solution(15035032497074455445)
XLA Ops:
  0.0 0.0 copy-start
  0.0 0.0 copy-start.1
  0.0 1.2 %pack_rows.1 = f32[20,8,128]{2,1,0:T(8,128)S(1)} custom-call(f32[2,32,128,128]{3,2,1,0:T(8,128)} %psi.5, s32[32,128,128]{2,1,0:T(8,128)} %dis.3), custom_call_target="tpu_custom_call" | custom-call | flops 8192 | bytes 114688 | tf_op jit(solution)/shard_map/pack_rows/pallas_call | solution.py:547
  1.2 3.1 %collective-permute-start = (f32[20,8,128]{2,1,0:T(8,128)S(1)}, f32[20,8,128]{2,1,0:T(8,128)S(1)}, u32[]{:S(2)}, u32[]{:S(2)}) collective-permute-start(f32[20,8,128]{2,1,0:T(8,128)S(1)} %pack_rows.1), channel_id=1, source_target_pairs={{0,2},{1,3},{2,0},{3,1},{4,6},{5,7},{6,4},{7,5},{8,9},{9,8},{10,12... | collective-permute-start | bytes 245768 | tf_op jit(solution)/shard_map/ppermute | solution.py:582
  4.3 0.0 copy-done
  4.3 0.0 copy-done.1
  4.3 2.3 %pack_columns.1 = (f32[12,128,128]{2,1,0:T(8,128)S(1)}, f32[3,128,128]{2,1,0:T(8,128)S(1)}, f32[128,128]{1,0:T(8,128)S(1)}) custom-call(f32[2,32,128,128]{3,2,1,0:T(8,128)S(1)} %copy-done, s32[32,128,128]{2,1,0:T(8,128)S(1)} %copy-done.1), custom_call_target="tpu_custom_call" | custom-call | flops 1572864 | bytes 2752512 | tf_op jit(solution)/shard_map/pack_columns/pallas_call | solution.py:547
  6.6 0.1 collective-permute-done.got
  6.7 0.0 collective-permute-start.1
  6.7 1.3 %slopes.1 = (f32[2,14,144,128]{3,2,1,0:T(8,128)S(1)}, f32[2,12,144,128]{3,2,1,0:T(8,128)S(1)}, f32[2,12,144,128]{3,2,1,0:T(8,128)S(1)}, f32[8,6,112,128]{3,2,1,0:T(8,128)S(1)}) custom-call(f32[2,32,128,128]{3,2,1,0:T(8,128)S(1)} %copy-done, f32[12,128,128]{2,1,0:T(8,128)S(1)} %get-tuple-element.27.pot), custom_call_target="tpu_custom_call" | custom-call | flops 7864320 | bytes 3670016 | tf_op jit(solution)/shard_map/slopes/pallas_call | solution.py:547
  8.0 0.0 collective-permute-done.1.other
  8.0 0.2 %pack_corners.1 = (f32[3,8,128]{2,1,0:T(8,128)S(1)}, f32[136,128]{1,0:T(8,128)S(1)}) custom-call(f32[20,8,128]{2,1,0:T(8,128)S(1)} %collective-permute-done.got, f32[20,8,128]{2,1,0:T(8,128)S(1)} %collective-permute-done.1.other, f32[128,128]{1,0:T(8,128)S(1)} %get-tuple-element.40.refs_0_), custom_call_target="tpu_custom_call" | custom-call | flops 16384 | bytes 57344 | tf_op jit(solution)/shard_map/pack_corners/pallas_call | solution.py:547
  8.2 2.0 %collective-permute-start.2 = (f32[136,128]{1,0:T(8,128)S(1)}, f32[136,128]{1,0:T(8,128)S(1)}, u32[]{:S(2)}, u32[]{:S(2)}) collective-permute-start(f32[136,128]{1,0:T(8,128)S(1)} %get-tuple-element.42), channel_id=1, source_target_pairs={{0,1},{2,3},{4,5},{6,7},{1,0},{3,2},{5,4},{7,6},{8,9},{10,11},{12,... | collective-permute-start | bytes 208904 | tf_op jit(solution)/shard_map/ppermute | solution.py:560
  10.2 3.4 %step.1 = (f32[2,8,128,128]{3,2,1,0:T(8,128)S(1)}, f32[2,14,144,128]{3,2,1,0:T(8,128)S(1)}, f32[2,12,144,128]{3,2,1,0:T(8,128)S(1)}, f32[2,12,144,128]{3,2,1,0:T(8,128)S(1)}) custom-call(f32[12,128,128]{2,1,0:T(8,128)S(1)} %get-tuple-element.27.pot, ...), custom_call_target="tpu_custom_call", output_to_operand_aliasing={{1}: (4, {}), {2}: (5, {}), {3}: (6, {})} | custom-call | flops 31457280 | bytes 3670016 | tf_op jit(solution)/shard_map/step/pallas_call | solution.py:547
  13.6 0.0 collective-permute-done.2.refs_2_
  13.6 1.8 %strips.1 = f32[2,8,128,128]{3,2,1,0:T(8,128)} custom-call(f32[2,8,128,128]{3,2,1,0:T(8,128)S(1)} %get-tuple-element.38.part, f32[3,128,128]{2,1,0:T(8,128)S(1)} %get-tuple-element.39.refs_0_, f32[3,8,128]{2,1,0:T(8,128)S(1)} %get-tuple-element.41.refs_1_, f32[136,128]{1,0:T(8,128)S(1)} %collective-permute-done.2.refs_2_), custom_call_target="tpu_custom_call" | custom-call | flops 3932160 | bytes 1835008 | tf_op jit(solution)/shard_map/strips/pallas_call | solution.py:547
Async XLA Ops:
  0.0 4.3 %copy-start = (f32[2,32,128,128]{3,2,1,0:T(8,128)S(1)}, f32[2,32,128,128]{3,2,1,0:T(8,128)}, u32[]{:S(2)}) copy-start(f32[2,32,128,128]{3,2,1,0:T(8,128)} %psi.5) | copy-start | bytes 12582916
  0.0 4.3 %copy-start.1 = (s32[32,128,128]{2,1,0:T(8,128)S(1)}, s32[32,128,128]{2,1,0:T(8,128)}, u32[]{:S(2)}) copy-start(s32[32,128,128]{2,1,0:T(8,128)} %dis.3) | copy-start | bytes 6291460
  1.2 5.5 %collective-permute-start = (f32[20,8,128]{2,1,0:T(8,128)S(1)}, f32[20,8,128]{2,1,0:T(8,128)S(1)}, u32[]{:S(2)}, u32[]{:S(2)}) collective-permute-start(f32[20,8,128]{2,1,0:T(8,128)S(1)} %pack_rows.1), channel_id=1, source_target_pairs={{0,2},{1,3},{2,0},{3,1},{4,6},{5,7},{6,4},{7,5},{8,9},{9,8},{10,12... | collective-permute-start | bytes 245768 | tf_op jit(solution)/shard_map/ppermute | solution.py:582
  6.7 1.3 %collective-permute-start.1 = (f32[20,8,128]{2,1,0:T(8,128)S(1)}, f32[20,8,128]{2,1,0:T(8,128)S(1)}, u32[]{:S(2)}, u32[]{:S(2)}) collective-permute-start(f32[20,8,128]{2,1,0:T(8,128)S(1)} %collective-permute-done.got), channel_id=1, source_target_pairs={{0,8},{8,0},{16,24},{24,16},{1,9},{9,1},{17,25},{25,17},{2,10},{10... | collective-permute-start | bytes 245768 | tf_op jit(solution)/shard_map/ppermute | solution.py:592
  8.2 5.4 %collective-permute-start.2 = (f32[136,128]{1,0:T(8,128)S(1)}, f32[136,128]{1,0:T(8,128)S(1)}, u32[]{:S(2)}, u32[]{:S(2)}) collective-permute-start(f32[136,128]{1,0:T(8,128)S(1)} %get-tuple-element.42), channel_id=1, source_target_pairs={{0,1},{2,3},{4,5},{6,7},{1,0},{3,2},{5,4},{7,6},{8,9},{10,11},{12,... | collective-permute-start | bytes 208904 | tf_op jit(solution)/shard_map/ppermute | solution.py:560
